TPU v7x, 256 devices: a whole 4x4x8 slice. The times are simulated.
256 devices in a mesh: prow: 8 (over x, y_hi), pcol: 32 (over y_lo, z, core).
Axes of the slice: x: 4, y: 4 (y_hi: 2, y_lo: 2; y = y_hi * 2 + y_lo), z: 8, core: 2. Of those that a mesh axis runs over, the one named last changes fastest.
Arguments:
- anc_inverse: float32 [8192, 8192], P('pcol', 'prow'), may hold values from -8 to 8
- lpanel: float32 [8192, 2, 2048], P('prow', None, 'pcol'), may hold values from -6 to 6
- pattern: int32 [2, 16], replicated, may hold values from 0 to 31, as said below
Outputs:
- selected: float32 [8192, 2, 2048], P('pcol', None, 'prow')
Inputs may be any that keep to these rules, and one draw needn't show every extreme that they name: `pattern`: entry q of each row is block 2q or block 2q + 1, so each row names one block of every aligned pair of blocks, in rising order, always the first and the last block.
All inputs are finite; a program needn't handle non-finite values.
Results may differ from a plain program's by a relative error of at most 0.00007.
Values sent between devices are 32-bit elements; how exact they have to be, the bound alone decides.
No kernel may reach another device: no remote copies, remote signals or barrier semaphores. Data moves between devices by JAX's collectives and lax.ppermute only.
A program may use at most 64 MiB of HBM per device.

v0:
```python
import jax
import jax.numpy as jnp
from jax import lax
from jax.sharding import PartitionSpec as P

B = 256


def pattern_mask(first, count, pattern):
    block_ids = (first + lax.broadcasted_iota(jnp.int32, (count, 1, 1), 0)) // B
    return jnp.any(block_ids == pattern[None, :, :], axis=2).astype(jnp.float32)


def columns_product(coeffs, form):

    def multiply(piece, start):
        return jnp.einsum(form, coeffs, piece, precision=lax.Precision.HIGHEST)

    return multiply


def per_device(anc_inverse, lpanel, pattern):
    rows_here, cols_here = anc_inverse.shape
    row_first = lax.axis_index("pcol") * rows_here
    col_first = lax.axis_index("prow") * cols_here
    row_mask = pattern_mask(row_first, rows_here, pattern)
    col_mask = pattern_mask(col_first, cols_here, pattern)
    operand = lpanel * col_mask[:, :, None]
    form = "rc,ckw->rkw"
    multiply = columns_product(anc_inverse, form)
    partial_value = multiply(lax.all_gather(operand, "pcol", axis=2, tiled=True), jnp.int32(0))
    summed = lax.psum_scatter(partial_value, "prow", scatter_dimension=2, tiled=True)
    return -(summed * row_mask[:, :, None])


def solution(mesh):
    return jax.shard_map(
        per_device,
        mesh=mesh,
        in_specs=(P("pcol", "prow"), P("prow", None, "pcol"), P()),
        out_specs=P("pcol", None, "prow"),
        check_vma=False,
    )
```

profile of v0, /device:TPU:1, one launch (start us, length us, event | category | flops | bytes accessed | tf_op | source)
XLA Modules:
  0.0 229.1 jit_solution(8855517315177436655)
XLA Ops:
  6.5 0.0 copy-start
  6.5 0.0 copy-start.1
  6.5 0.0 all-gather.2.cloned.1.call-start
  6.6 0.9 compare_reduce_fusion
  7.4 1.9 broadcast_multiply_fusion
  9.3 0.0 all-gather.2.cloned.1.call-update
  9.4 0.0 reduce-scatter.2.cloned.1.call-start
  9.4 104.1 %all-gather.2.cloned.1.call-done = f32[1024,2,2048]{0,2,1:T(8,128)} async-done(((f32[1024,2,64]{0,2,1:T(8,128)}), f32[1024,2,2048]{0,2,1:T(8,128)}) %all-gather.2.cloned.1.call-update) | async-done | bytes 16777232 | tf_op jit(solution)/shard_map/all_gather | solution.py:31
  113.5 0.0 copy-done
  113.5 17.7 %convolution_bitcast_fusion = f32[256,2,2048]{0,2,1:T(8,128)} fusion(f32[1024,2,2048]{0,2,1:T(8,128)} %all-gather.2.cloned.1.call-done, f32[256,1024]{1,0:T(8,128)S(1)} %copy-done), kind=kOutput, calls=%fused_computation | convolution fusion | flops 12884901888 | bytes 22020096 | tf_op jit(solution)/shard_map/rc,ckw->rkw/dot_general | solution.py:17
  131.2 0.0 reduce-scatter.2.cloned.1.call-update
  131.3 0.0 copy-done.1
  131.3 0.1 compare_reduce_fusion.1
  131.4 88.8 %reduce-scatter.2.cloned.1.call-done = f32[256,2,256]{0,2,1:T(8,128)} async-done(((f32[256,2,2048]{0,2,1:T(8,128)}), f32[256,2,256]{0,2,1:T(8,128)}) %reduce-scatter.2.cloned.1.call-update) | async-done | bytes 524304 | tf_op jit(solution)/shard_map/reduce_scatter | solution.py:32
  220.2 1.1 multiply_negate_fusion
  221.2 1.0 copy.5
  (4 shorter events, 0.0 us)
Async XLA Ops:
  6.5 106.9 %copy-start = (f32[256,1024]{1,0:T(8,128)S(1)}, f32[256,1024]{1,0:T(8,128)}, u32[]{:S(2)}) copy-start(f32[256,1024]{1,0:T(8,128)} %param.3) | copy-start | bytes 3145732
  6.5 124.7 %copy-start.1 = (s32[2,16]{1,0:T(2,128)S(1)}, s32[2,16]{1,0:T(2,128)}, u32[]{:S(2)}) copy-start(s32[2,16]{1,0:T(2,128)} %param.5) | copy-start | bytes 388
  6.5 106.9 %all-gather.2.cloned.1.call-start = ((), (), s32[]{:S(2)}) async-start(), calls=%async_computation.1 | async-start | bytes 17301504 | tf_op jit(solution)/shard_map/all_gather | solution.py:31
  9.4 210.8 %reduce-scatter.2.cloned.1.call-start = ((), (), s32[]{:S(2)}) async-start(), calls=%async_computation.2 | async-start | bytes 4718592 | tf_op jit(solution)/shard_map/reduce_scatter | solution.py:32
Sparse Core Ops, SparseCore 0:
  9.5 103.9 all-gather.1
  131.4 88.7 reduce-scatter.1
where the time goes:
time: 229 us
  waiting for transfers between devices  193 us (84%)
  matrix products  17.7 us (8%)
  between operations  13.4 us (6%)
  other arithmetic  3.96 us (2%)
    all_gather x1, waiting for transfers between devices, per_device(): lax.all_gather(operand, 'pcol', axis=2, tiled=True)  104 us
    reduce_scatter x1, waiting for transfers between devices, per_device(): lax.psum_scatter(partial_value, 'prow', scatter_dimension=2, tiled=True)  88.8 us
    dot_general x1, matrix products, multiply(): return jnp.einsum(form, coeffs, piece, precision=lax.Precision.HIGHEST)  17.7 us
  transfers between devices with their start and end apart: 2, of which 2 were waited for; matrix products, arithmetic and copies ran while one was open for 0% of the time, Pallas kernels for 0%

commit v1 on v0

v1 whole, which is shorter than its diff:
```python
import jax
import jax.numpy as jnp
from jax import lax
from jax.experimental import pallas as pl
from jax.experimental.pallas import tpu as pltpu
from jax.sharding import PartitionSpec as P

B = 256
H = 128
F32 = jnp.float32
BF16 = jnp.bfloat16
AXES = ("prow", "pcol")
VMEM_LIMIT = 40 * 1024 * 1024

DEVICES = [(x, y, z, c) for x in range(4) for y in range(4) for z in range(8) for c in range(2)]


def number(x, y, z, c):
    return (2 * x + y // 2) * 32 + 16 * (y % 2) + 2 * z + c


def send(array, move):
    pairs = [(number(*d), number(*move(*d))) for d in DEVICES]
    return lax.ppermute(array, AXES, pairs)


def other_core(x, y, z, c):
    return x, y, z, 1 - c


def other_low(x, y, z, c):
    return x, y ^ 1, z, c


def other_high(x, y, z, c):
    return x, y ^ 2, z, c


def other_both(x, y, z, c):
    return x, y ^ 3, z, c


def ring(x, y, z, c):
    return x, y, (z + 1 - 2 * c) % 8, c


def along_x(step):
    return lambda x, y, z, c: ((x + step) % 4, y, z, c)


def home(x, y, z, c):
    child, low = y // 2, y % 2
    return 2 * low + x // 2, 2 * (x % 2) + c, z, child


def position():
    prow, pcol = lax.axis_index("prow"), lax.axis_index("pcol")
    return prow % 2, pcol // 16, (pcol // 2) % 8, pcol % 2, prow, pcol


def call(kernel, shapes, *args, flops=0):
    in_specs = [
        pl.BlockSpec(memory_space=pltpu.SMEM if a.dtype == jnp.int32 else pltpu.VMEM) for a in args
    ]
    shapes = [jax.ShapeDtypeStruct(s, d) for s, d in shapes]
    size = sum(a.size * a.dtype.itemsize for a in (*args, *shapes))
    return pl.pallas_call(
        kernel,
        out_shape=shapes,
        in_specs=in_specs,
        out_specs=[pl.BlockSpec(memory_space=pltpu.VMEM) for _ in shapes],
        compiler_params=pltpu.CompilerParams(vmem_limit_bytes=VMEM_LIMIT),
        cost_estimate=pl.CostEstimate(flops=flops, bytes_accessed=size, transcendentals=0),
    )(*args)


def column(pattern_ref, child, prow, t):
    block = pattern_ref[child, 2 * prow + t] - 4 * prow
    return pl.multiple_of(block * B, B)


def compact_panel(pattern_ref, panel_ref, mine_ref, other_ref):
    child, _, _, _, prow, _ = position()
    for out_ref, which in ((mine_ref, child), (other_ref, 1 - child)):
        for t in range(2):
            start = column(pattern_ref, which, prow, t)
            out_ref[:, t * B:(t + 1) * B] = panel_ref[which, :, pl.ds(start, B)]


def compact_inverse(pattern_ref, inverse_ref, keep_ref, give_ref):
    _, _, _, core, prow, _ = position()
    for out_ref, half in ((keep_ref, core), (give_ref, 1 - core)):
        rows = pl.ds(pl.multiple_of(half * H, H), H)
        for child in range(2):
            for t in range(2):
                start = column(pattern_ref, child, prow, t)
                out_ref[child, :, t * B:(t + 1) * B] = inverse_ref[rows, pl.ds(start, B)]


def choose_rows(pattern_ref, own_ref, got_ref, mine_ref, other_ref):
    child, _, _, core, _, pcol = position()
    pair = pcol // 2
    for out_ref, which in ((mine_ref, child), (other_ref, 1 - child)):
        here = pattern_ref[which, pair] - 2 * pair == core

        @pl.when(here)
        def _():
            out_ref[...] = own_ref[which]

        @pl.when(jnp.logical_not(here))
        def _():
            out_ref[...] = got_ref[which]


def split(value):
    high = value.astype(BF16)
    return high, (value - high.astype(F32)).astype(BF16)


def split_inverse(*refs):
    own, got, (high_ref, low_ref) = refs[:4], refs[4:8], refs[8:]
    _, low_y, _, core, _, _ = position()
    for half_refs, half in ((own, core), (got, 1 - core)):
        rows = pl.ds(pl.multiple_of(half * H, H), H)
        for i, ref in enumerate(half_refs):
            side = (low_y + core + i // 2) % 2
            high, low = split(ref[...])
            columns = slice((i % 2) * 2 * B, (i % 2 + 1) * 2 * B)
            high_ref[side, rows, columns] = high
            low_ref[side, rows, columns] = low


def dot(a, b):
    return lax.dot_general(a, b, (((1,), (1,)), ((), ())), preferred_element_type=F32)


def multiply(counts, *refs):
    n = len(counts)
    pieces, (high_ref, low_ref, keep_ref, give_ref) = refs[:2 * n], refs[2 * n:]
    slot = 0
    for i, count in enumerate(counts):
        parts = [split(ref[:64 * count]) for ref in pieces[2 * i:2 * i + 2]]
        for side, out_ref in enumerate((keep_ref, give_ref)):
            total = None
            for j, (high, low) in enumerate(parts):
                columns = slice(j * 2 * B, (j + 1) * 2 * B)
                a_high, a_low = high_ref[side, :, columns], low_ref[side, :, columns]
                term = dot(high, a_high) + (dot(high, a_low) + dot(low, a_high))
                total = term if total is None else total + term
            out_ref[slot:slot + count] = total.reshape(count, 64, B)
        slot += count


def product(counts, pieces, a_high, a_low):
    rows = sum(counts)
    shape = ((rows, 64, B), F32)
    return call(
        lambda *refs: multiply(counts, *refs),
        [shape, shape],
        *pieces,
        a_high,
        a_low,
        flops=2 * rows * 64 * 2 * B * 4 * B * 3,
    )


def arrange(own_early, own_late, got_early, got_late, *outs):
    _, _, z, core, prow, _ = position()
    x = prow // 2
    early = own_early.shape[0]
    for m, out_ref in enumerate(outs):
        for odd in range(2):
            z_from = 2 * ((x + m) % 4) + odd
            ahead = (z - z_from + 8) % 8
            for w_core in range(2):
                near = jnp.logical_or(ahead == 0, ahead == 4)
                source = jnp.where(near, w_core, jnp.where(ahead < 4, 0, 1))
                steps = jnp.where(ahead <= 4, ahead, 8 - ahead)
                inner = 2 * steps - 1 + jnp.where(source == w_core, 0, 1)
                slot = jnp.where(ahead == 0, 0, inner)
                here = source == core
                first = slot < early
                for ref, mine, start in (
                    (own_early, True, 0), (own_late, True, early), (got_early, False, 0), (got_late, False, early),
                ):
                    wanted = jnp.logical_and(here == mine, first == (start == 0))

                    @pl.when(wanted)
                    def _():
                        out_ref[2 * odd + w_core] = ref[slot - start]


def per_device(anc_inverse, lpanel, pattern):
    panel = jnp.transpose(lpanel, (1, 2, 0))
    half_piece = ((64, 2 * B), F32)
    mine, other = call(compact_panel, [half_piece, half_piece], pattern, panel)
    swapped = send(other, other_high)
    mine = jnp.concatenate([mine, send(mine, other_core)], axis=0)
    chain_a = [mine]

    pair = ((2, H, 2 * B), F32)
    keep, give = call(compact_inverse, [pair, pair], pattern, anc_inverse)
    got = send(give, other_core)
    quarter = ((H, 2 * B), F32)
    a_mine, a_other = call(choose_rows, [quarter, quarter], pattern, keep, got)

    chain_b = [jnp.concatenate([swapped, send(swapped, other_core)], axis=0)]
    for step in range(3):
        chain_a.append(send(chain_a[-1], ring))
        chain_b.append(send(chain_b[-1], ring))
    chain_a.append(send(chain_a[-1][:64], ring))
    chain_b.append(send(chain_b[-1][:64], ring))

    blocks = [a_mine, send(a_other, other_high), send(a_mine, other_low), send(a_other, other_both)]
    halves = [send(block, other_core) for block in blocks]
    whole = ((2, B, 4 * B), BF16)
    a_high, a_low = call(split_inverse, [whole, whole], *blocks, *halves)

    chunks = [piece for both in zip(chain_a, chain_b) for piece in both]
    keep_early, give_early = product((1, 2, 2), chunks[:6], a_high, a_low)
    keep_late, give_late = product((2, 1), chunks[6:], a_high, a_low)
    got_early = send(give_early, other_core)
    got_late = send(give_late, other_core)
    terms = call(arrange, [((4, 64, B), F32)] * 4, keep_early, keep_late, got_early, got_late)
    total = terms[0]
    for m in range(1, 4):
        total = total + send(terms[m], along_x(m))
    result = send(total, home).reshape(B, B)
    second = send(result, other_core)

    _, _, _, core, _, pcol = position()
    block = pcol
    members = jnp.any(pattern == block, axis=1)
    both = jnp.where(core == 0, jnp.stack([result, second]), jnp.stack([second, result]))
    both = jnp.where(members[:, None, None], -both, 0.0)
    return jnp.transpose(both, (2, 0, 1))


def solution(mesh):
    return jax.shard_map(
        per_device,
        mesh=mesh,
        in_specs=(P("pcol", "prow"), P("prow", None, "pcol"), P()),
        out_specs=P("pcol", None, "prow"),
        check_vma=False,
    )
```

time: 229 us -> 91.6 us (0.40)
  the two profiles are of different devices: /device:TPU:1 before, /device:TPU:3 now
where the time goes in v1:
time: 91.6 us; the launch traced here: 91.4 us
  waiting for transfers between devices  42.4 us (46%)
  starting transfers between devices  35.6 us (39%)
  Pallas kernels  7.85 us (9%)
  local copies, waits for them, and re-layouts  3.47 us (4%)
  other arithmetic  1.87 us (2%)
    ppermute x26, waiting for transfers between devices, send(): return lax.ppermute(array, AXES, pairs)  42.4 us
    ppermute x26, starting transfers between devices, send(): return lax.ppermute(array, AXES, pairs)  35.6 us
    pallas_call x7, Pallas kernels, call(): pl.pallas_call(kernel, out_shape=shapes, in_specs=in_specs, out_specs=[pl...  7.85 us
    unnamed x8, local copies, waits for them, and re-layouts  2.96 us
  transfers between devices with their start and end apart: 26, of which 12 were waited for; matrix products, arithmetic and copies ran while one was open for 0% of the time, Pallas kernels for 7%

profile of v1, /device:TPU:3, one launch (start us, length us, event | category | flops | bytes accessed | tf_op | source)
XLA Modules:
  0.0 91.4 jit_solution(10227188296285324205)
XLA Ops:
  0.0 0.7 copy-done.2
  0.7 1.0 %copy-done.1 = f32[1024,2,64]{0,2,1:T(8,128)S(1)} copy-done((f32[1024,2,64]{0,2,1:T(8,128)S(1)}, f32[1024,2,64]{0,2,1:T(8,128)}, u32[]{:S(2)}) %copy-start.1) | copy-done | bytes 524312
  1.7 0.6 shard_map.37
  2.3 0.8 collective-permute-start
  3.1 1.2 %copy-done = f32[256,1024]{1,0:T(8,128)S(1)} copy-done((f32[256,1024]{1,0:T(8,128)S(1)}, f32[256,1024]{1,0:T(8,128)}, u32[]{:S(2)}) %copy-start) | copy-done | bytes 1048600
  4.3 0.6 shard_map.38
  4.9 0.1 collective-permute-start.7
  5.1 3.0 %collective-permute-start.1 = (f32[64,512]{1,0:T(8,128)S(1)}, f32[64,512]{1,0:T(8,128)S(1)}, u32[]{:S(2)}, u32[]{:S(2)}) collective-permute-start(f32[64,512]{1,0:T(8,128)S(1)} %get-tuple-element.22), channel_id=1, source_target_pairs={{0,32},{1,33},{2,34},{3,35},{4,36},{5,37},{6,38},{7,39},{8,40},{9,... | collective-permute-start | bytes 393224 | tf_op jit(solution)/shard_map/ppermute | solution.py:24
  8.1 5.7 %collective-permute-start.3 = (f32[128,512]{1,0:T(8,128)S(1)}, f32[128,512]{1,0:T(8,128)S(1)}, u32[]{:S(2)}, u32[]{:S(2)}) collective-permute-start(f32[128,512]{1,0:T(8,128)S(1)} %constant_dynamic-update-slice_fusion.refs_0_), channel_id=1, source_target_pairs={{0,2},{1,15},{2,4},{3,1},{4,6},{5,3},{6,8},{7,5},{8,10},{9,7},{10,... | collective-permute-start | bytes 786440 | tf_op jit(solution)/shard_map/ppermute | solution.py:24
  13.8 1.3 %collective-permute-done.2 = f32[64,512]{1,0:T(8,128)S(1)} collective-permute-done((f32[64,512]{1,0:T(8,128)S(1)}, f32[64,512]{1,0:T(8,128)S(1)}, u32[]{:S(2)}, u32[]{:S(2)}) %collective-permute-start.2) | collective-permute-done | bytes 131104 | tf_op jit(solution)/shard_map/ppermute | solution.py:24
  15.1 4.1 %collective-permute-start.4 = (f32[128,512]{1,0:T(8,128)S(1)}, f32[128,512]{1,0:T(8,128)S(1)}, u32[]{:S(2)}, u32[]{:S(2)}) collective-permute-start(f32[128,512]{1,0:T(8,128)S(1)} %constant_dynamic-update-slice_fusion.2.refs_1_), channel_id=1, source_target_pairs={{0,2},{1,15},{2,4},{3,1},{4,6},{5,3},{6,8},{7,5},{8,10},{9,7},{10,... | collective-permute-start | bytes 786440 | tf_op jit(solution)/shard_map/ppermute | solution.py:24
  19.2 1.0 %collective-permute-start.5 = (f32[128,512]{1,0:T(8,128)S(1)}, f32[128,512]{1,0:T(8,128)S(1)}, u32[]{:S(2)}, u32[]{:S(2)}) collective-permute-start(f32[128,512]{1,0:T(8,128)S(1)} %collective-permute-done.3.refs_2_), channel_id=1, source_target_pairs={{0,2},{1,15},{2,4},{3,1},{4,6},{5,3},{6,8},{7,5},{8,10},{9,7},{10,... | collective-permute-start | bytes 786440 | tf_op jit(solution)/shard_map/ppermute | solution.py:24
  20.2 2.3 %collective-permute-done.4.refs_3_ = f32[128,512]{1,0:T(8,128)S(1)} collective-permute-done((f32[128,512]{1,0:T(8,128)S(1)}, f32[128,512]{1,0:T(8,128)S(1)}, u32[]{:S(2)}, u32[]{:S(2)}) %collective-permute-start.4) | collective-permute-done | bytes 262176 | tf_op jit(solution)/shard_map/ppermute | solution.py:24
  22.5 3.1 %collective-permute-start.6 = (f32[128,512]{1,0:T(8,128)S(1)}, f32[128,512]{1,0:T(8,128)S(1)}, u32[]{:S(2)}, u32[]{:S(2)}) collective-permute-start(f32[128,512]{1,0:T(8,128)S(1)} %collective-permute-done.4.refs_3_), channel_id=1, source_target_pairs={{0,2},{1,15},{2,4},{3,1},{4,6},{5,3},{6,8},{7,5},{8,10},{9,7},{10,... | collective-permute-start | bytes 786440 | tf_op jit(solution)/shard_map/ppermute | solution.py:24
  25.6 0.6 shard_map.39
  26.3 1.4 %collective-permute-start.9 = (f32[128,512]{1,0:T(8,128)S(1)}, f32[128,512]{1,0:T(8,128)S(1)}, u32[]{:S(2)}, u32[]{:S(2)}) collective-permute-start(f32[128,512]{1,0:T(8,128)S(1)} %get-tuple-element.25.refs_0_), channel_id=1, source_target_pairs={{0,16},{1,17},{2,18},{3,19},{4,20},{5,21},{6,22},{7,23},{8,24},{9,... | collective-permute-start | bytes 786440 | tf_op jit(solution)/shard_map/ppermute | solution.py:24
  27.7 2.6 %collective-permute-start.8 = (f32[128,512]{1,0:T(8,128)S(1)}, f32[128,512]{1,0:T(8,128)S(1)}, u32[]{:S(2)}, u32[]{:S(2)}) collective-permute-start(f32[128,512]{1,0:T(8,128)S(1)} %get-tuple-element.26), channel_id=1, source_target_pairs={{0,32},{1,33},{2,34},{3,35},{4,36},{5,37},{6,38},{7,39},{8,40},{9,... | collective-permute-start | bytes 786440 | tf_op jit(solution)/shard_map/ppermute | solution.py:24
  30.3 1.8 %collective-permute-start.16 = (f32[128,512]{1,0:T(8,128)S(1)}, f32[128,512]{1,0:T(8,128)S(1)}, u32[]{:S(2)}, u32[]{:S(2)}) collective-permute-start(f32[128,512]{1,0:T(8,128)S(1)} %collective-permute-done.6.refs_5_), channel_id=1, source_target_pairs={{0,2},{1,15},{2,4},{3,1},{4,6},{5,3},{6,8},{7,5},{8,10},{9,7},{10,... | collective-permute-start | bytes 786440 | tf_op jit(solution)/shard_map/ppermute | solution.py:24
  32.1 2.6 %collective-permute-done.9.refs_2_ = f32[128,512]{1,0:T(8,128)S(1)} collective-permute-done((f32[128,512]{1,0:T(8,128)S(1)}, f32[128,512]{1,0:T(8,128)S(1)}, u32[]{:S(2)}, u32[]{:S(2)}) %collective-permute-start.9) | collective-permute-done | bytes 262176 | tf_op jit(solution)/shard_map/ppermute | solution.py:24
  34.7 6.9 %collective-permute-done.8.refs_1_ = f32[128,512]{1,0:T(8,128)S(1)} collective-permute-done((f32[128,512]{1,0:T(8,128)S(1)}, f32[128,512]{1,0:T(8,128)S(1)}, u32[]{:S(2)}, u32[]{:S(2)}) %collective-permute-start.8) | collective-permute-done | bytes 262176 | tf_op jit(solution)/shard_map/ppermute | solution.py:24
  41.6 3.1 %collective-permute-done.10.refs_3_ = f32[128,512]{1,0:T(8,128)S(1)} collective-permute-done((f32[128,512]{1,0:T(8,128)S(1)}, f32[128,512]{1,0:T(8,128)S(1)}, u32[]{:S(2)}, u32[]{:S(2)}) %collective-permute-start.10) | collective-permute-done | bytes 262176 | tf_op jit(solution)/shard_map/ppermute | solution.py:24
  44.7 0.4 collective-permute-start.12
  45.1 0.2 collective-permute-start.14
  45.3 0.7 collective-permute-start.17
  46.0 0.8 collective-permute-start.18
  46.8 0.3 shard_map.40
  47.1 3.1 %shard_map.41 = (f32[5,64,256]{2,1,0:T(8,128)S(1)}, f32[5,64,256]{2,1,0:T(8,128)S(1)}) custom-call(f32[128,512]{1,0:T(8,128)S(1)} %constant_dynamic-update-slice_fusion.refs_0_, f32[128,512]{1,0:T(8,128)S(1)} %constant_dynamic-update-slice_fusion.2.refs_1_, f32[128,512]{1,0:T(8,128)S(1)} %collective-permute-done.3.refs_2_, ...), custom_call_target="tpu_custom_call" | custom-call | flops 1006632960 | bytes 4325376 | tf_op jit(solution)/shard_map/pallas_call | solution.py:67
  50.2 0.3 collective-permute-start.19
  50.5 0.3 collective-permute-done.18.refs_3_
  50.9 2.1 %shard_map.42 = (f32[3,64,256]{2,1,0:T(8,128)S(1)}, f32[3,64,256]{2,1,0:T(8,128)S(1)}) custom-call(f32[128,512]{1,0:T(8,128)S(1)} %collective-permute-done.15.refs_0_, f32[128,512]{1,0:T(8,128)S(1)} %collective-permute-done.16.refs_1_, f32[64,512]{1,0:T(8,128)S(1)} %collective-permute-done.17.refs_2_, f32[64,512]{1,0:T(8,128)S(1)} %collective-permute-done.18.refs_3_, ...), custom_call_target="tpu_custom_call" | custom-call | flops 603979776 | bytes 3276800 | tf_op jit(solution)/shard_map/pallas_call | solution.py:67
  52.9 2.5 %collective-permute-start.20 = (f32[3,64,256]{2,1,0:T(8,128)S(1)}, f32[3,64,256]{2,1,0:T(8,128)S(1)}, u32[]{:S(2)}, u32[]{:S(2)}) collective-permute-start(f32[3,64,256]{2,1,0:T(8,128)S(1)} %get-tuple-element.32), channel_id=1, source_target_pairs={{0,1},{1,0},{2,3},{3,2},{4,5},{5,4},{6,7},{7,6},{8,9},{9,8},{10,11... | collective-permute-start | bytes 589832 | tf_op jit(solution)/shard_map/ppermute | solution.py:24
  55.4 1.1 %collective-permute-done.20.got_late = f32[3,64,256]{2,1,0:T(8,128)S(1)} collective-permute-done((f32[3,64,256]{2,1,0:T(8,128)S(1)}, f32[3,64,256]{2,1,0:T(8,128)S(1)}, u32[]{:S(2)}, u32[]{:S(2)}) %collective-permute-start.20) | collective-permute-done | bytes 196640 | tf_op jit(solution)/shard_map/ppermute | solution.py:24
  56.5 0.5 shard_map.43
  57.0 1.3 %collective-permute-start.21 = (f32[4,64,256]{2,1,0:T(8,128)S(1)}, f32[4,64,256]{2,1,0:T(8,128)S(1)}, u32[]{:S(2)}, u32[]{:S(2)}) collective-permute-start(f32[4,64,256]{2,1,0:T(8,128)S(1)} %get-tuple-element.34), channel_id=1, source_target_pairs={{0,64},{1,65},{2,66},{3,67},{4,68},{5,69},{6,70},{7,71},{8,72},{9,... | collective-permute-start | bytes 786440 | tf_op jit(solution)/shard_map/ppermute | solution.py:24
  58.3 0.8 collective-permute-start.22
  59.1 1.9 %collective-permute-start.23 = (f32[4,64,256]{2,1,0:T(8,128)S(1)}, f32[4,64,256]{2,1,0:T(8,128)S(1)}, u32[]{:S(2)}, u32[]{:S(2)}) collective-permute-start(f32[4,64,256]{2,1,0:T(8,128)S(1)} %get-tuple-element.36), channel_id=1, source_target_pairs={{0,192},{1,193},{2,194},{3,195},{4,196},{5,197},{6,198},{7,199},{8... | collective-permute-start | bytes 786440 | tf_op jit(solution)/shard_map/ppermute | solution.py:24
  61.0 3.6 %collective-permute-done.21 = f32[4,64,256]{2,1,0:T(8,128)S(1)} collective-permute-done((f32[4,64,256]{2,1,0:T(8,128)S(1)}, f32[4,64,256]{2,1,0:T(8,128)S(1)}, u32[]{:S(2)}, u32[]{:S(2)}) %collective-permute-start.21) | collective-permute-done | bytes 262176 | tf_op jit(solution)/shard_map/ppermute | solution.py:24
  64.6 2.5 %collective-permute-done.22 = f32[4,64,256]{2,1,0:T(8,128)S(1)} collective-permute-done((f32[4,64,256]{2,1,0:T(8,128)S(1)}, f32[4,64,256]{2,1,0:T(8,128)S(1)}, u32[]{:S(2)}, u32[]{:S(2)}) %collective-permute-start.22) | collective-permute-done | bytes 262176 | tf_op jit(solution)/shard_map/ppermute | solution.py:24
  67.1 5.2 %collective-permute-done.23 = f32[4,64,256]{2,1,0:T(8,128)S(1)} collective-permute-done((f32[4,64,256]{2,1,0:T(8,128)S(1)}, f32[4,64,256]{2,1,0:T(8,128)S(1)}, u32[]{:S(2)}, u32[]{:S(2)}) %collective-permute-start.23) | collective-permute-done | bytes 262176 | tf_op jit(solution)/shard_map/ppermute | solution.py:24
  72.3 3.0 %collective-permute-start.24 = (f32[4,64,256]{2,1,0:T(8,128)S(1)}, f32[4,64,256]{2,1,0:T(8,128)S(1)}, u32[]{:S(2)}, u32[]{:S(2)}) collective-permute-start(f32[4,64,256]{2,1,0:T(8,128)S(1)} %add_add_fusion), channel_id=1, source_target_pairs={{0,0},{1,16},{2,2},{3,18},{4,4},{5,20},{6,6},{7,22},{8,8},{9,24},{... | collective-permute-start | bytes 786440 | tf_op jit(solution)/shard_map/ppermute | solution.py:24
  75.3 12.4 %collective-permute-done.24 = f32[4,64,256]{2,1,0:T(8,128)S(1)} collective-permute-done((f32[4,64,256]{2,1,0:T(8,128)S(1)}, f32[4,64,256]{2,1,0:T(8,128)S(1)}, u32[]{:S(2)}, u32[]{:S(2)}) %collective-permute-start.24) | collective-permute-done | bytes 262176 | tf_op jit(solution)/shard_map/ppermute | solution.py:24
  87.7 0.1 copy.4
  87.9 0.4 collective-permute-start.25
  88.3 0.1 compare_reduce_fusion
  88.4 0.2 copy.5
  88.5 1.0 %collective-permute-done.25 = f32[256,256]{0,1:T(8,128)S(1)} collective-permute-done((f32[256,256]{0,1:T(8,128)S(1)}, f32[256,256]{0,1:T(8,128)S(1)}, u32[]{:S(2)}, u32[]{:S(2)}) %collective-permute-start.25) | collective-permute-done | bytes 262176 | tf_op jit(solution)/shard_map/ppermute | solution.py:24
  89.5 0.2 stack.10
  89.7 1.7 %fusion.2 = f32[256,2,256]{2,1,0:T(2,128)} fusion(f32[1,256,256]{1,0,2:T(1,128)S(1)} %stack.10, f32[1,256,256]{1,0,2:T(1,128)S(1)} %copy.5, pred[2]{0:T(512)(128)(4,1)S(1)} %compare_reduce_fusion, pred[]{:T(512)S(6)} %eq.13), kind=kLoop, calls=%fused_computation.3 | loop fusion | flops 655360 | bytes 1048579 | tf_op jit(solution)/shard_map/transpose | solution.py:236
  (29 shorter events, 0.2 us)
Async XLA Ops:
  0.0 0.7 copy-start.2
  0.7 1.0 %copy-start.1 = (f32[1024,2,64]{0,2,1:T(8,128)S(1)}, f32[1024,2,64]{0,2,1:T(8,128)}, u32[]{:S(2)}) copy-start(f32[1024,2,64]{0,2,1:T(8,128)} %param.4) | copy-start | bytes 1572868
  2.3 5.7 %collective-permute-start = (f32[64,512]{1,0:T(8,128)S(1)}, f32[64,512]{1,0:T(8,128)S(1)}, u32[]{:S(2)}, u32[]{:S(2)}) collective-permute-start(f32[64,512]{1,0:T(8,128)S(1)} %get-tuple-element.21), channel_id=1, source_target_pairs={{0,1},{1,0},{2,3},{3,2},{4,5},{5,4},{6,7},{7,6},{8,9},{9,8},{10,11... | collective-permute-start | bytes 393224 | tf_op jit(solution)/shard_map/ppermute | solution.py:24
  3.1 1.2 %copy-start = (f32[256,1024]{1,0:T(8,128)S(1)}, f32[256,1024]{1,0:T(8,128)}, u32[]{:S(2)}) copy-start(f32[256,1024]{1,0:T(8,128)} %inverse_ref.1) | copy-start | bytes 3145732
  4.9 20.7 %collective-permute-start.7 = (f32[2,128,512]{2,1,0:T(8,128)S(1)}, f32[2,128,512]{2,1,0:T(8,128)S(1)}, u32[]{:S(2)}, u32[]{:S(2)}) collective-permute-start(f32[2,128,512]{2,1,0:T(8,128)S(1)} %get-tuple-element.24), channel_id=1, source_target_pairs={{0,1},{1,0},{2,3},{3,2},{4,5},{5,4},{6,7},{7,6},{8,9},{9,8},{10,11... | collective-permute-start | bytes 1572872 | tf_op jit(solution)/shard_map/ppermute | solution.py:24
  5.1 8.7 %collective-permute-start.1 = (f32[64,512]{1,0:T(8,128)S(1)}, f32[64,512]{1,0:T(8,128)S(1)}, u32[]{:S(2)}, u32[]{:S(2)}) collective-permute-start(f32[64,512]{1,0:T(8,128)S(1)} %get-tuple-element.22), channel_id=1, source_target_pairs={{0,32},{1,33},{2,34},{3,35},{4,36},{5,37},{6,38},{7,39},{8,40},{9,... | collective-permute-start | bytes 393224 | tf_op jit(solution)/shard_map/ppermute | solution.py:24
  8.1 11.1 %collective-permute-start.3 = (f32[128,512]{1,0:T(8,128)S(1)}, f32[128,512]{1,0:T(8,128)S(1)}, u32[]{:S(2)}, u32[]{:S(2)}) collective-permute-start(f32[128,512]{1,0:T(8,128)S(1)} %constant_dynamic-update-slice_fusion.refs_0_), channel_id=1, source_target_pairs={{0,2},{1,15},{2,4},{3,1},{4,6},{5,3},{6,8},{7,5},{8,10},{9,7},{10,... | collective-permute-start | bytes 786440 | tf_op jit(solution)/shard_map/ppermute | solution.py:24
  13.7 1.3 %collective-permute-start.2 = (f32[64,512]{1,0:T(8,128)S(1)}, f32[64,512]{1,0:T(8,128)S(1)}, u32[]{:S(2)}, u32[]{:S(2)}) collective-permute-start(f32[64,512]{1,0:T(8,128)S(1)} %collective-permute-done.1), channel_id=1, source_target_pairs={{0,1},{1,0},{2,3},{3,2},{4,5},{5,4},{6,7},{7,6},{8,9},{9,8},{10,11... | collective-permute-start | bytes 393224 | tf_op jit(solution)/shard_map/ppermute | solution.py:24
  15.1 7.4 %collective-permute-start.4 = (f32[128,512]{1,0:T(8,128)S(1)}, f32[128,512]{1,0:T(8,128)S(1)}, u32[]{:S(2)}, u32[]{:S(2)}) collective-permute-start(f32[128,512]{1,0:T(8,128)S(1)} %constant_dynamic-update-slice_fusion.2.refs_1_), channel_id=1, source_target_pairs={{0,2},{1,15},{2,4},{3,1},{4,6},{5,3},{6,8},{7,5},{8,10},{9,7},{10,... | collective-permute-start | bytes 786440 | tf_op jit(solution)/shard_map/ppermute | solution.py:24
  19.2 11.1 %collective-permute-start.5 = (f32[128,512]{1,0:T(8,128)S(1)}, f32[128,512]{1,0:T(8,128)S(1)}, u32[]{:S(2)}, u32[]{:S(2)}) collective-permute-start(f32[128,512]{1,0:T(8,128)S(1)} %collective-permute-done.3.refs_2_), channel_id=1, source_target_pairs={{0,2},{1,15},{2,4},{3,1},{4,6},{5,3},{6,8},{7,5},{8,10},{9,7},{10,... | collective-permute-start | bytes 786440 | tf_op jit(solution)/shard_map/ppermute | solution.py:24
  22.5 7.8 %collective-permute-start.6 = (f32[128,512]{1,0:T(8,128)S(1)}, f32[128,512]{1,0:T(8,128)S(1)}, u32[]{:S(2)}, u32[]{:S(2)}) collective-permute-start(f32[128,512]{1,0:T(8,128)S(1)} %collective-permute-done.4.refs_3_), channel_id=1, source_target_pairs={{0,2},{1,15},{2,4},{3,1},{4,6},{5,3},{6,8},{7,5},{8,10},{9,7},{10,... | collective-permute-start | bytes 786440 | tf_op jit(solution)/shard_map/ppermute | solution.py:24
  26.3 8.4 %collective-permute-start.9 = (f32[128,512]{1,0:T(8,128)S(1)}, f32[128,512]{1,0:T(8,128)S(1)}, u32[]{:S(2)}, u32[]{:S(2)}) collective-permute-start(f32[128,512]{1,0:T(8,128)S(1)} %get-tuple-element.25.refs_0_), channel_id=1, source_target_pairs={{0,16},{1,17},{2,18},{3,19},{4,20},{5,21},{6,22},{7,23},{8,24},{9,... | collective-permute-start | bytes 786440 | tf_op jit(solution)/shard_map/ppermute | solution.py:24
  27.7 13.9 %collective-permute-start.8 = (f32[128,512]{1,0:T(8,128)S(1)}, f32[128,512]{1,0:T(8,128)S(1)}, u32[]{:S(2)}, u32[]{:S(2)}) collective-permute-start(f32[128,512]{1,0:T(8,128)S(1)} %get-tuple-element.26), channel_id=1, source_target_pairs={{0,32},{1,33},{2,34},{3,35},{4,36},{5,37},{6,38},{7,39},{8,40},{9,... | collective-permute-start | bytes 786440 | tf_op jit(solution)/shard_map/ppermute | solution.py:24
  30.3 14.4 %collective-permute-start.10 = (f32[128,512]{1,0:T(8,128)S(1)}, f32[128,512]{1,0:T(8,128)S(1)}, u32[]{:S(2)}, u32[]{:S(2)}) collective-permute-start(f32[128,512]{1,0:T(8,128)S(1)} %get-tuple-element.26), channel_id=1, source_target_pairs={{0,48},{1,49},{2,50},{3,51},{4,52},{5,53},{6,54},{7,55},{8,56},{9,... | collective-permute-start | bytes 786440 | tf_op jit(solution)/shard_map/ppermute | solution.py:24
  30.3 14.8 %collective-permute-start.15 = (f32[128,512]{1,0:T(8,128)S(1)}, f32[128,512]{1,0:T(8,128)S(1)}, u32[]{:S(2)}, u32[]{:S(2)}) collective-permute-start(f32[128,512]{1,0:T(8,128)S(1)} %collective-permute-done.5.refs_4_), channel_id=1, source_target_pairs={{0,2},{1,15},{2,4},{3,1},{4,6},{5,3},{6,8},{7,5},{8,10},{9,7},{10,... | collective-permute-start | bytes 786440 | tf_op jit(solution)/shard_map/ppermute | solution.py:24
  30.3 14.9 %collective-permute-start.16 = (f32[128,512]{1,0:T(8,128)S(1)}, f32[128,512]{1,0:T(8,128)S(1)}, u32[]{:S(2)}, u32[]{:S(2)}) collective-permute-start(f32[128,512]{1,0:T(8,128)S(1)} %collective-permute-done.6.refs_5_), channel_id=1, source_target_pairs={{0,2},{1,15},{2,4},{3,1},{4,6},{5,3},{6,8},{7,5},{8,10},{9,7},{10,... | collective-permute-start | bytes 786440 | tf_op jit(solution)/shard_map/ppermute | solution.py:24
  34.7 11.3 %collective-permute-start.11 = (f32[128,512]{1,0:T(8,128)S(1)}, f32[128,512]{1,0:T(8,128)S(1)}, u32[]{:S(2)}, u32[]{:S(2)}) collective-permute-start(f32[128,512]{1,0:T(8,128)S(1)} %get-tuple-element.25.refs_0_), channel_id=1, source_target_pairs={{0,1},{1,0},{2,3},{3,2},{4,5},{5,4},{6,7},{7,6},{8,9},{9,8},{10,11... | collective-permute-start | bytes 786440 | tf_op jit(solution)/shard_map/ppermute | solution.py:24
  41.6 5.2 %collective-permute-start.13 = (f32[128,512]{1,0:T(8,128)S(1)}, f32[128,512]{1,0:T(8,128)S(1)}, u32[]{:S(2)}, u32[]{:S(2)}) collective-permute-start(f32[128,512]{1,0:T(8,128)S(1)} %collective-permute-done.9.refs_2_), channel_id=1, source_target_pairs={{0,1},{1,0},{2,3},{3,2},{4,5},{5,4},{6,7},{7,6},{8,9},{9,8},{10,11... | collective-permute-start | bytes 786440 | tf_op jit(solution)/shard_map/ppermute | solution.py:24
  44.7 2.0 %collective-permute-start.12 = (f32[128,512]{1,0:T(8,128)S(1)}, f32[128,512]{1,0:T(8,128)S(1)}, u32[]{:S(2)}, u32[]{:S(2)}) collective-permute-start(f32[128,512]{1,0:T(8,128)S(1)} %collective-permute-done.8.refs_1_), channel_id=1, source_target_pairs={{0,1},{1,0},{2,3},{3,2},{4,5},{5,4},{6,7},{7,6},{8,9},{9,8},{10,11... | collective-permute-start | bytes 786440 | tf_op jit(solution)/shard_map/ppermute | solution.py:24
  45.1 1.7 %collective-permute-start.14 = (f32[128,512]{1,0:T(8,128)S(1)}, f32[128,512]{1,0:T(8,128)S(1)}, u32[]{:S(2)}, u32[]{:S(2)}) collective-permute-start(f32[128,512]{1,0:T(8,128)S(1)} %collective-permute-done.10.refs_3_), channel_id=1, source_target_pairs={{0,1},{1,0},{2,3},{3,2},{4,5},{5,4},{6,7},{7,6},{8,9},{9,8},{10,11... | collective-permute-start | bytes 786440 | tf_op jit(solution)/shard_map/ppermute | solution.py:24
  45.3 5.3 %collective-permute-start.17 = (f32[64,512]{1,0:T(8,128)S(1)}, f32[64,512]{1,0:T(8,128)S(1)}, u32[]{:S(2)}, u32[]{:S(2)}) collective-permute-start(f32[64,512]{1,0:T(8,128)S(1)} %slice.8), channel_id=1, source_target_pairs={{0,2},{1,15},{2,4},{3,1},{4,6},{5,3},{6,8},{7,5},{8,10},{9,7},{10,... | collective-permute-start | bytes 393224 | tf_op jit(solution)/shard_map/ppermute | solution.py:24
  46.0 4.9 %collective-permute-start.18 = (f32[64,512]{1,0:T(8,128)S(1)}, f32[64,512]{1,0:T(8,128)S(1)}, u32[]{:S(2)}, u32[]{:S(2)}) collective-permute-start(f32[64,512]{1,0:T(8,128)S(1)} %slice.9), channel_id=1, source_target_pairs={{0,2},{1,15},{2,4},{3,1},{4,6},{5,3},{6,8},{7,5},{8,10},{9,7},{10,... | collective-permute-start | bytes 393224 | tf_op jit(solution)/shard_map/ppermute | solution.py:24
  50.2 6.3 %collective-permute-start.19 = (f32[5,64,256]{2,1,0:T(8,128)S(1)}, f32[5,64,256]{2,1,0:T(8,128)S(1)}, u32[]{:S(2)}, u32[]{:S(2)}) collective-permute-start(f32[5,64,256]{2,1,0:T(8,128)S(1)} %get-tuple-element.31), channel_id=1, source_target_pairs={{0,1},{1,0},{2,3},{3,2},{4,5},{5,4},{6,7},{7,6},{8,9},{9,8},{10,11... | collective-permute-start | bytes 983048 | tf_op jit(solution)/shard_map/ppermute | solution.py:24
  52.9 3.6 %collective-permute-start.20 = (f32[3,64,256]{2,1,0:T(8,128)S(1)}, f32[3,64,256]{2,1,0:T(8,128)S(1)}, u32[]{:S(2)}, u32[]{:S(2)}) collective-permute-start(f32[3,64,256]{2,1,0:T(8,128)S(1)} %get-tuple-element.32), channel_id=1, source_target_pairs={{0,1},{1,0},{2,3},{3,2},{4,5},{5,4},{6,7},{7,6},{8,9},{9,8},{10,11... | collective-permute-start | bytes 589832 | tf_op jit(solution)/shard_map/ppermute | solution.py:24
  57.0 7.6 %collective-permute-start.21 = (f32[4,64,256]{2,1,0:T(8,128)S(1)}, f32[4,64,256]{2,1,0:T(8,128)S(1)}, u32[]{:S(2)}, u32[]{:S(2)}) collective-permute-start(f32[4,64,256]{2,1,0:T(8,128)S(1)} %get-tuple-element.34), channel_id=1, source_target_pairs={{0,64},{1,65},{2,66},{3,67},{4,68},{5,69},{6,70},{7,71},{8,72},{9,... | collective-permute-start | bytes 786440 | tf_op jit(solution)/shard_map/ppermute | solution.py:24
  58.3 8.8 %collective-permute-start.22 = (f32[4,64,256]{2,1,0:T(8,128)S(1)}, f32[4,64,256]{2,1,0:T(8,128)S(1)}, u32[]{:S(2)}, u32[]{:S(2)}) collective-permute-start(f32[4,64,256]{2,1,0:T(8,128)S(1)} %get-tuple-element.35), channel_id=1, source_target_pairs={{0,128},{1,129},{2,130},{3,131},{4,132},{5,133},{6,134},{7,135},{8... | collective-permute-start | bytes 786440 | tf_op jit(solution)/shard_map/ppermute | solution.py:24
  59.1 13.1 %collective-permute-start.23 = (f32[4,64,256]{2,1,0:T(8,128)S(1)}, f32[4,64,256]{2,1,0:T(8,128)S(1)}, u32[]{:S(2)}, u32[]{:S(2)}) collective-permute-start(f32[4,64,256]{2,1,0:T(8,128)S(1)} %get-tuple-element.36), channel_id=1, source_target_pairs={{0,192},{1,193},{2,194},{3,195},{4,196},{5,197},{6,198},{7,199},{8... | collective-permute-start | bytes 786440 | tf_op jit(solution)/shard_map/ppermute | solution.py:24
  72.3 15.4 %collective-permute-start.24 = (f32[4,64,256]{2,1,0:T(8,128)S(1)}, f32[4,64,256]{2,1,0:T(8,128)S(1)}, u32[]{:S(2)}, u32[]{:S(2)}) collective-permute-start(f32[4,64,256]{2,1,0:T(8,128)S(1)} %add_add_fusion), channel_id=1, source_target_pairs={{0,0},{1,16},{2,2},{3,18},{4,4},{5,20},{6,6},{7,22},{8,8},{9,24},{... | collective-permute-start | bytes 786440 | tf_op jit(solution)/shard_map/ppermute | solution.py:24
  87.9 1.6 %collective-permute-start.25 = (f32[256,256]{0,1:T(8,128)S(1)}, f32[256,256]{0,1:T(8,128)S(1)}, u32[]{:S(2)}, u32[]{:S(2)}) collective-permute-start(f32[256,256]{0,1:T(8,128)S(1)} %copy.4), channel_id=1, source_target_pairs={{0,1},{1,0},{2,3},{3,2},{4,5},{5,4},{6,7},{7,6},{8,9},{9,8},{10,11... | collective-permute-start | bytes 786440 | tf_op jit(solution)/shard_map/ppermute | solution.py:24

commit v2 on v1

v2 whole, which is shorter than its diff:
```python
import jax
import jax.numpy as jnp
from jax import lax
from jax.experimental import pallas as pl
from jax.experimental.pallas import tpu as pltpu
from jax.sharding import PartitionSpec as P

B = 256
H = 128
F32 = jnp.float32
BF16 = jnp.bfloat16
AXES = ("prow", "pcol")
VMEM_LIMIT = 40 * 1024 * 1024

DEVICES = [(x, y, z, c) for x in range(4) for y in range(4) for z in range(8) for c in range(2)]


def number(x, y, z, c):
    return (2 * x + y // 2) * 32 + 16 * (y % 2) + 2 * z + c


def send(array, move):
    pairs = [(number(*d), number(*move(*d))) for d in DEVICES]
    return lax.ppermute(array, AXES, pairs)


def other_core(x, y, z, c):
    return x, y, z, 1 - c


def other_low(x, y, z, c):
    return x, y ^ 1, z, c


def other_high(x, y, z, c):
    return x, y ^ 2, z, c


def other_both(x, y, z, c):
    return x, y ^ 3, z, c


def ring(x, y, z, c):
    return x, y, (z + 1 - 2 * c) % 8, c


def along_x(step):
    return lambda x, y, z, c: ((x + step) % 4, y, z, c)


def spread(flip):
    return lambda x, y, z, c: (x, 2 * (y // 2 ^ flip) + c, z, y % 2)


def position():
    prow, pcol = lax.axis_index("prow"), lax.axis_index("pcol")
    return prow % 2, pcol // 16, (pcol // 2) % 8, pcol % 2, prow, pcol


def call(kernel, shapes, *args, flops=0):
    in_specs = [
        pl.BlockSpec(memory_space=pltpu.SMEM if a.dtype == jnp.int32 else pltpu.VMEM) for a in args
    ]
    shapes = [jax.ShapeDtypeStruct(s, d) for s, d in shapes]
    size = sum(a.size * a.dtype.itemsize for a in (*args, *shapes))
    return pl.pallas_call(
        kernel,
        out_shape=shapes,
        in_specs=in_specs,
        out_specs=[pl.BlockSpec(memory_space=pltpu.VMEM) for _ in shapes],
        compiler_params=pltpu.CompilerParams(vmem_limit_bytes=VMEM_LIMIT),
        cost_estimate=pl.CostEstimate(flops=flops, bytes_accessed=size, transcendentals=0),
    )(*args)


def column(pattern_ref, child, prow, t):
    block = pattern_ref[child, 2 * prow + t] - 4 * prow
    return pl.multiple_of(block * B, B)


def compact_panel(pattern_ref, panel_ref, mine_ref, other_ref):
    child, _, _, _, prow, _ = position()
    for out_ref, which in ((mine_ref, child), (other_ref, 1 - child)):
        for t in range(2):
            start = column(pattern_ref, which, prow, t)
            out_ref[:, t * B:(t + 1) * B] = panel_ref[which, :, pl.ds(start, B)]


def compact_inverse(pattern_ref, inverse_ref, keep_ref, give_ref):
    _, _, _, core, prow, _ = position()
    for out_ref, half in ((keep_ref, core), (give_ref, 1 - core)):
        rows = pl.ds(pl.multiple_of(half * H, H), H)
        for child in range(2):
            for t in range(2):
                start = column(pattern_ref, child, prow, t)
                out_ref[child, :, t * B:(t + 1) * B] = inverse_ref[rows, pl.ds(start, B)]


def choose_rows(pattern_ref, own_ref, got_ref, mine_ref, other_ref):
    child, _, _, core, _, pcol = position()
    pair = pcol // 2
    for out_ref, which in ((mine_ref, child), (other_ref, 1 - child)):
        here = pattern_ref[which, pair] - 2 * pair == core

        @pl.when(here)
        def _():
            out_ref[...] = own_ref[which]

        @pl.when(jnp.logical_not(here))
        def _():
            out_ref[...] = got_ref[which]


def split(value):
    high = value.astype(BF16)
    return high, (value - high.astype(F32)).astype(BF16)


def split_inverse(*refs):
    own, got, (high_ref, low_ref) = refs[:4], refs[4:8], refs[8:]
    _, low_y, _, core, _, _ = position()
    for half_refs, half in ((own, core), (got, 1 - core)):
        for i, ref in enumerate(half_refs):
            side = (low_y + core + i // 2) % 2
            high, low = split(ref[...].T)
            rows = slice((i % 2) * 2 * B, (i % 2 + 1) * 2 * B)
            columns = pl.ds(pl.multiple_of(side * B + half * H, H), H)
            high_ref[rows, columns] = high
            low_ref[rows, columns] = low


def dot(a, b):
    return jnp.dot(a, b, preferred_element_type=F32)


def multiply(counts, *refs):
    n = len(counts)
    pieces, (high_ref, low_ref, keep_ref, give_ref) = refs[:2 * n], refs[2 * n:]
    slots = sum(counts)
    total = None
    for j in range(2):
        parts = [ref[:count].reshape(64 * count, 2 * B) for count, ref in zip(counts, pieces[j::2])]
        high, low = split(jnp.concatenate(parts, axis=0))
        rows = slice(j * 2 * B, (j + 1) * 2 * B)
        a_high, a_low = high_ref[rows], low_ref[rows]
        term = dot(high, a_high) + (dot(high, a_low) + dot(low, a_high))
        total = term if total is None else total + term
    keep_ref[...] = total[:, :B].reshape(slots, 64, B)
    give_ref[...] = total[:, B:].reshape(slots, 64, B)


def product(pieces, a_high, a_low):
    counts = tuple(piece.shape[0] for piece in pieces[::2])
    slots = sum(counts)
    shape = ((slots, 64, B), F32)
    return call(
        lambda *refs: multiply(counts, *refs),
        [shape, shape],
        *pieces,
        a_high,
        a_low,
        flops=2 * slots * 64 * 2 * B * 4 * B * 3,
    )


def arrange(own_early, own_late, got_early, got_late, *outs):
    child, _, z, core, prow, _ = position()
    x = prow // 2
    early = own_early.shape[0]
    for i, out_ref in enumerate(outs):
        m, flip = i // 2, 1 - i % 2
        target = (x + m) % 4
        w_low = target // 2
        for odd in range(2):
            z_from = 4 * (target % 2) + 2 * (child + flip - 2 * child * flip) + odd
            ahead = (z - z_from + 8) % 8
            near = jnp.logical_or(ahead == 0, ahead == 4)
            source = jnp.where(near, w_low, jnp.where(ahead < 4, 0, 1))
            steps = jnp.where(ahead <= 4, ahead, 8 - ahead)
            inner = 2 * steps - 1 + jnp.where(source == w_low, 0, 1)
            slot = jnp.where(ahead == 0, 0, inner)
            here = source == core
            first = slot < early
            for ref, mine, start in (
                (own_early, True, 0), (own_late, True, early), (got_early, False, 0), (got_late, False, early),
            ):
                wanted = jnp.logical_and(here == mine, first == (start == 0))

                @pl.when(wanted)
                def _():
                    out_ref[odd] = ref[slot - start]


def finish(pattern_ref, own_flip, own_same, got_flip, got_same, out_ref):
    high, _, _, core, _, pcol = position()
    pair = pcol // 2
    for child in range(2):
        here = pattern_ref[child, pair] - 2 * pair == core
        for flip, own, got in ((0, own_same, got_same), (1, own_flip, got_flip)):
            active = (high + child) % 2 == flip

            @pl.when(jnp.logical_and(here, active))
            def _():
                for odd in range(2):
                    mine, theirs = own[odd], got[odd]
                    first = jnp.where(core == 0, mine, theirs)
                    second = jnp.where(core == 0, theirs, mine)
                    block = jnp.concatenate([first, second], axis=0)
                    out_ref[:, child, odd * H:(odd + 1) * H] = -block.T

        @pl.when(jnp.logical_not(here))
        def _():
            out_ref[:, child, :] = jnp.zeros((B, B), F32)


def after(value, *others):
    return lax.optimization_barrier((value, *others))[0]


def per_device(anc_inverse, lpanel, pattern):
    panel = jnp.transpose(lpanel, (1, 2, 0))
    half_piece = ((64, 2 * B), F32)
    mine, other = call(compact_panel, [half_piece, half_piece], pattern, panel)
    columns = [send(mine, spread(0)), send(other, spread(1))]

    pair = ((2, H, 2 * B), F32)
    keep, give = call(compact_inverse, [pair, pair], pattern, anc_inverse)
    got = send(give, other_core)
    quarter = ((H, 2 * B), F32)
    a_mine, a_other = call(choose_rows, [quarter, quarter], pattern, keep, got)
    blocks = [a_mine, send(a_other, other_high), send(a_mine, other_low), send(a_other, other_both)]

    columns = lax.optimization_barrier(columns + [a_mine])[:2]
    pairs = lax.optimization_barrier([jnp.stack([part, send(part, other_core)]) for part in columns])
    early = [pairs[0][:1], pairs[1][:1]]
    for step in range(3):
        if step:
            pairs[0] = after(pairs[0], blocks[step])
        pairs = [send(part, ring) for part in pairs]
        early += pairs
    last = send(jnp.concatenate([part[:1] for part in pairs]), ring)
    late = [last[:1], last[1:]]

    blocks[3] = after(blocks[3], *pairs)
    halves = [send(block, other_core) for block in blocks]
    whole = ((4 * B, 2 * B), BF16)
    a_high, a_low = call(split_inverse, [whole, whole], *blocks, *halves)
    keep_early, give_early = product(early, a_high, a_low)
    keep_late, give_late = product(late, a_high, a_low)
    got_early = send(after(give_early, last), other_core)
    got_late = send(give_late, other_core)
    terms = call(arrange, [((2, 64, B), F32)] * 8, keep_early, keep_late, got_early, got_late)
    moved = list(terms[:2]) + [send(terms[2 * m + i], along_x(m)) for i in range(2) for m in range(1, 4)]
    result = [moved[i] + moved[2 + 3 * i] + moved[3 + 3 * i] + moved[4 + 3 * i] for i in range(2)]
    result = [send(result[0], spread(1)), send(result[1], spread(0))]
    second = [send(part, other_core) for part in result]
    return call(finish, [((B, 2, B), F32)], pattern, *result, *second)[0]


def solution(mesh):
    return jax.shard_map(
        per_device,
        mesh=mesh,
        in_specs=(P("pcol", "prow"), P("prow", None, "pcol"), P()),
        out_specs=P("pcol", None, "prow"),
        check_vma=False,
    )
```

time: 91.6 us -> 83.3 us (0.909)
  the two profiles are of different devices: /device:TPU:3 before, /device:TPU:1 now
where the time goes in v2:
time: 83.3 us; the launch traced here: 83.1 us
  starting transfers between devices  48.8 us (59%)
  waiting for transfers between devices  25.1 us (30%)
  Pallas kernels  6.84 us (8%)
  local copies, waits for them, and re-layouts  1.97 us (2%)
    ppermute x31, starting transfers between devices, send(): return lax.ppermute(array, AXES, pairs)  48.8 us
    ppermute x31, waiting for transfers between devices, send(): return lax.ppermute(array, AXES, pairs)  25.1 us
    pallas_call x8, Pallas kernels, call(): pl.pallas_call(kernel, out_shape=shapes, in_specs=in_specs, out_specs=[pl...  6.84 us
    unnamed x8, local copies, waits for them, and re-layouts  1.91 us
  transfers between devices with their start and end apart: 31, of which 15 were waited for; matrix products, arithmetic and copies ran while one was open for 0% of the time, Pallas kernels for 5%

profile of v2, /device:TPU:1, one launch (start us, length us, event | category | flops | bytes accessed | tf_op | source)
XLA Modules:
  0.0 83.1 jit_solution(5732379224089641851)
XLA Ops:
  0.0 1.2 %copy-done = f32[256,1024]{1,0:T(8,128)S(1)} copy-done((f32[256,1024]{1,0:T(8,128)S(1)}, f32[256,1024]{1,0:T(8,128)}, u32[]{:S(2)}) %copy-start) | copy-done | bytes 1048600
  1.2 0.7 copy-done.2
  1.9 0.6 shard_map.38
  2.6 3.3 %collective-permute-start.2 = (f32[2,128,512]{2,1,0:T(8,128)S(1)}, f32[2,128,512]{2,1,0:T(8,128)S(1)}, u32[]{:S(2)}, u32[]{:S(2)}) collective-permute-start(f32[2,128,512]{2,1,0:T(8,128)S(1)} %get-tuple-element.36), channel_id=1, source_target_pairs={{0,1},{1,0},{2,3},{3,2},{4,5},{5,4},{6,7},{7,6},{8,9},{9,8},{10,11... | collective-permute-start | bytes 1572872 | tf_op jit(solution)/shard_map/ppermute | solution.py:24
  5.9 0.6 shard_map.37
  6.5 1.9 %collective-permute-start = (f32[64,512]{1,0:T(8,128)S(1)}, f32[64,512]{1,0:T(8,128)S(1)}, u32[]{:S(2)}, u32[]{:S(2)}) collective-permute-start(f32[64,512]{1,0:T(8,128)S(1)} %get-tuple-element.33), channel_id=1, source_target_pairs={{0,0},{1,16},{2,2},{3,18},{4,4},{5,20},{6,6},{7,22},{8,8},{9,24},{... | collective-permute-start | bytes 393224 | tf_op jit(solution)/shard_map/ppermute | solution.py:24
  8.4 1.8 %collective-permute-start.1 = (f32[64,512]{1,0:T(8,128)S(1)}, f32[64,512]{1,0:T(8,128)S(1)}, u32[]{:S(2)}, u32[]{:S(2)}) collective-permute-start(f32[64,512]{1,0:T(8,128)S(1)} %get-tuple-element.34), channel_id=1, source_target_pairs={{0,32},{1,48},{2,34},{3,50},{4,36},{5,52},{6,38},{7,54},{8,40},{9,... | collective-permute-start | bytes 393224 | tf_op jit(solution)/shard_map/ppermute | solution.py:24
  10.2 0.6 shard_map.39
  10.9 2.2 %collective-permute-done = f32[64,512]{1,0:T(8,128)S(1)} collective-permute-done((f32[64,512]{1,0:T(8,128)S(1)}, f32[64,512]{1,0:T(8,128)S(1)}, u32[]{:S(2)}, u32[]{:S(2)}) %collective-permute-start) | collective-permute-done | bytes 131104 | tf_op jit(solution)/shard_map/ppermute | solution.py:24
  13.1 2.1 %collective-permute-done.1 = f32[64,512]{1,0:T(8,128)S(1)} collective-permute-done((f32[64,512]{1,0:T(8,128)S(1)}, f32[64,512]{1,0:T(8,128)S(1)}, u32[]{:S(2)}, u32[]{:S(2)}) %collective-permute-start.1) | collective-permute-done | bytes 131104 | tf_op jit(solution)/shard_map/ppermute | solution.py:24
  15.3 0.3 collective-permute-start.4
  15.6 1.1 %collective-permute-start.7 = (f32[128,512]{1,0:T(8,128)S(1)}, f32[128,512]{1,0:T(8,128)S(1)}, u32[]{:S(2)}, u32[]{:S(2)}) collective-permute-start(f32[128,512]{1,0:T(8,128)S(1)} %get-tuple-element.42), channel_id=1, source_target_pairs={{0,32},{1,33},{2,34},{3,35},{4,36},{5,37},{6,38},{7,39},{8,40},{9,... | collective-permute-start | bytes 786440 | tf_op jit(solution)/shard_map/ppermute | solution.py:24
  16.8 5.6 %collective-permute-start.5 = (f32[2,64,512]{2,1,0:T(8,128)S(1)}, f32[2,64,512]{2,1,0:T(8,128)S(1)}, u32[]{:S(2)}, u32[]{:S(2)}) collective-permute-start(f32[2,64,512]{2,1,0:T(8,128)S(1)} %pad_maximum_fusion), channel_id=1, source_target_pairs={{0,2},{1,15},{2,4},{3,1},{4,6},{5,3},{6,8},{7,5},{8,10},{9,7},{10,... | collective-permute-start | bytes 786440 | tf_op jit(solution)/shard_map/ppermute | solution.py:24
  22.5 0.7 collective-permute-start.6
  23.2 0.3 collective-permute-start.10
  23.5 1.3 %collective-permute-done.7.refs_1_ = f32[128,512]{1,0:T(8,128)S(1)} collective-permute-done((f32[128,512]{1,0:T(8,128)S(1)}, f32[128,512]{1,0:T(8,128)S(1)}, u32[]{:S(2)}, u32[]{:S(2)}) %collective-permute-start.7) | collective-permute-done | bytes 262176 | tf_op jit(solution)/shard_map/ppermute | solution.py:24
  24.9 0.9 %collective-permute-done.5.refs_2_ = f32[2,64,512]{2,1,0:T(8,128)S(1)} collective-permute-done((f32[2,64,512]{2,1,0:T(8,128)S(1)}, f32[2,64,512]{2,1,0:T(8,128)S(1)}, u32[]{:S(2)}, u32[]{:S(2)}) %collective-permute-start.5) | collective-permute-done | bytes 262176 | tf_op jit(solution)/shard_map/ppermute | solution.py:24
  25.8 3.6 %collective-permute-start.8 = (f32[2,64,512]{2,1,0:T(8,128)S(1)}, f32[2,64,512]{2,1,0:T(8,128)S(1)}, u32[]{:S(2)}, u32[]{:S(2)}) collective-permute-start(f32[2,64,512]{2,1,0:T(8,128)S(1)} %collective-permute-done.5.refs_2_), channel_id=1, source_target_pairs={{0,2},{1,15},{2,4},{3,1},{4,6},{5,3},{6,8},{7,5},{8,10},{9,7},{10,... | collective-permute-start | bytes 786440 | tf_op jit(solution)/shard_map/ppermute | solution.py:24
  29.4 2.4 %collective-permute-start.9 = (f32[2,64,512]{2,1,0:T(8,128)S(1)}, f32[2,64,512]{2,1,0:T(8,128)S(1)}, u32[]{:S(2)}, u32[]{:S(2)}) collective-permute-start(f32[2,64,512]{2,1,0:T(8,128)S(1)} %collective-permute-done.6.refs_3_), channel_id=1, source_target_pairs={{0,2},{1,15},{2,4},{3,1},{4,6},{5,3},{6,8},{7,5},{8,10},{9,7},{10,... | collective-permute-start | bytes 786440 | tf_op jit(solution)/shard_map/ppermute | solution.py:24
  31.7 1.1 %collective-permute-start.13 = (f32[128,512]{1,0:T(8,128)S(1)}, f32[128,512]{1,0:T(8,128)S(1)}, u32[]{:S(2)}, u32[]{:S(2)}) collective-permute-start(f32[128,512]{1,0:T(8,128)S(1)} %get-tuple-element.42), channel_id=1, source_target_pairs={{0,48},{1,49},{2,50},{3,51},{4,52},{5,53},{6,54},{7,55},{8,56},{9,... | collective-permute-start | bytes 786440 | tf_op jit(solution)/shard_map/ppermute | solution.py:24
  32.9 2.9 %collective-permute-start.11 = (f32[2,64,512]{2,1,0:T(8,128)S(1)}, f32[2,64,512]{2,1,0:T(8,128)S(1)}, u32[]{:S(2)}, u32[]{:S(2)}) collective-permute-start(f32[2,64,512]{2,1,0:T(8,128)S(1)} %collective-permute-done.8.refs_4_), channel_id=1, source_target_pairs={{0,2},{1,15},{2,4},{3,1},{4,6},{5,3},{6,8},{7,5},{8,10},{9,7},{10,... | collective-permute-start | bytes 786440 | tf_op jit(solution)/shard_map/ppermute | solution.py:24
  35.8 3.1 %collective-permute-start.12 = (f32[2,64,512]{2,1,0:T(8,128)S(1)}, f32[2,64,512]{2,1,0:T(8,128)S(1)}, u32[]{:S(2)}, u32[]{:S(2)}) collective-permute-start(f32[2,64,512]{2,1,0:T(8,128)S(1)} %collective-permute-done.9.refs_5_), channel_id=1, source_target_pairs={{0,2},{1,15},{2,4},{3,1},{4,6},{5,3},{6,8},{7,5},{8,10},{9,7},{10,... | collective-permute-start | bytes 786440 | tf_op jit(solution)/shard_map/ppermute | solution.py:24
  38.9 0.5 collective-permute-start.15
  39.4 0.8 collective-permute-done.13.refs_3_
  40.2 2.0 %collective-permute-done.12.refs_7_ = f32[2,64,512]{2,1,0:T(8,128)S(1)} collective-permute-done((f32[2,64,512]{2,1,0:T(8,128)S(1)}, f32[2,64,512]{2,1,0:T(8,128)S(1)}, u32[]{:S(2)}, u32[]{:S(2)}) %collective-permute-start.12) | collective-permute-done | bytes 262176 | tf_op jit(solution)/shard_map/ppermute | solution.py:24
  42.2 3.3 %collective-permute-start.17 = (f32[128,512]{1,0:T(8,128)S(1)}, f32[128,512]{1,0:T(8,128)S(1)}, u32[]{:S(2)}, u32[]{:S(2)}) collective-permute-start(f32[128,512]{1,0:T(8,128)S(1)} %collective-permute-done.13.refs_3_), channel_id=1, source_target_pairs={{0,1},{1,0},{2,3},{3,2},{4,5},{5,4},{6,7},{7,6},{8,9},{9,8},{10,11... | collective-permute-start | bytes 786440 | tf_op jit(solution)/shard_map/ppermute | solution.py:24
  45.6 0.8 collective-permute-start.18
  46.7 0.6 shard_map.40
  47.3 1.6 %shard_map.41 = (f32[7,64,256]{2,1,0:T(8,128)S(1)}, f32[7,64,256]{2,1,0:T(8,128)S(1)}) custom-call(f32[1,64,512]{2,1,0:T(8,128)S(1)} %slice.18.refs_0_, f32[1,64,512]{2,1,0:T(8,128)S(1)} %slice.19.refs_1_, f32[2,64,512]{2,1,0:T(8,128)S(1)} %collective-permute-done.5.refs_2_, f32[2,64,512]{2,1,0:T(8,128)S(1)} %collective-permute-done.6.refs_3_, ...), custom_call_target="tpu_custom_call" | custom-call | flops 1409286144 | bytes 4849664 | tf_op jit(solution)/shard_map/pallas_call | solution.py:66
  48.9 2.5 %collective-permute-done.18 = f32[2,64,512]{2,1,0:T(8,128)S(1)} collective-permute-done((f32[2,64,512]{2,1,0:T(8,128)S(1)}, f32[2,64,512]{2,1,0:T(8,128)S(1)}, u32[]{:S(2)}, u32[]{:S(2)}) %collective-permute-start.18) | collective-permute-done | bytes 262176 | tf_op jit(solution)/shard_map/ppermute | solution.py:24
  51.4 2.1 %collective-permute-start.19 = (f32[7,64,256]{2,1,0:T(8,128)S(1)}, f32[7,64,256]{2,1,0:T(8,128)S(1)}, u32[]{:S(2)}, u32[]{:S(2)}) collective-permute-start(f32[7,64,256]{2,1,0:T(8,128)S(1)} %get-tuple-element.51), channel_id=1, source_target_pairs={{0,1},{1,0},{2,3},{3,2},{4,5},{5,4},{6,7},{7,6},{8,9},{9,8},{10,11... | collective-permute-start | bytes 1376264 | tf_op jit(solution)/shard_map/ppermute | solution.py:24
  53.5 0.6 shard_map.42
  54.2 1.2 %collective-permute-done.20.got_late = f32[1,64,256]{2,1,0:T(8,128)S(1)} collective-permute-done((f32[1,64,256]{2,1,0:T(8,128)S(1)}, f32[1,64,256]{2,1,0:T(8,128)S(1)}, u32[]{:S(2)}, u32[]{:S(2)}) %collective-permute-start.20) | collective-permute-done | bytes 65568 | tf_op jit(solution)/shard_map/ppermute | solution.py:24
  55.5 0.6 shard_map.43
  56.1 2.5 %collective-permute-start.23 = (f32[2,64,256]{2,1,0:T(8,128)S(1)}, f32[2,64,256]{2,1,0:T(8,128)S(1)}, u32[]{:S(2)}, u32[]{:S(2)}) collective-permute-start(f32[2,64,256]{2,1,0:T(8,128)S(1)} %get-tuple-element.56), channel_id=1, source_target_pairs={{0,192},{1,193},{2,194},{3,195},{4,196},{5,197},{6,198},{7,199},{8... | collective-permute-start | bytes 393224 | tf_op jit(solution)/shard_map/ppermute | solution.py:24
  58.6 0.5 collective-permute-start.22
  59.2 0.6 collective-permute-start.21
  59.8 2.1 %collective-permute-start.27 = (f32[2,64,256]{2,1,0:T(8,128)S(1)}, f32[2,64,256]{2,1,0:T(8,128)S(1)}, u32[]{:S(2)}, u32[]{:S(2)}) collective-permute-start(f32[2,64,256]{2,1,0:T(8,128)S(1)} %get-tuple-element.60), channel_id=1, source_target_pairs={{0,192},{1,193},{2,194},{3,195},{4,196},{5,197},{6,198},{7,199},{8... | collective-permute-start | bytes 393224 | tf_op jit(solution)/shard_map/ppermute | solution.py:24
  61.8 1.2 %collective-permute-start.26 = (f32[2,64,256]{2,1,0:T(8,128)S(1)}, f32[2,64,256]{2,1,0:T(8,128)S(1)}, u32[]{:S(2)}, u32[]{:S(2)}) collective-permute-start(f32[2,64,256]{2,1,0:T(8,128)S(1)} %get-tuple-element.59), channel_id=1, source_target_pairs={{0,128},{1,129},{2,130},{3,131},{4,132},{5,133},{6,134},{7,135},{8... | collective-permute-start | bytes 393224 | tf_op jit(solution)/shard_map/ppermute | solution.py:24
  63.1 0.8 collective-permute-done.23
  63.8 1.0 %collective-permute-done.22 = f32[2,64,256]{2,1,0:T(8,128)S(1)} collective-permute-done((f32[2,64,256]{2,1,0:T(8,128)S(1)}, f32[2,64,256]{2,1,0:T(8,128)S(1)}, u32[]{:S(2)}, u32[]{:S(2)}) %collective-permute-start.22) | collective-permute-done | bytes 131104 | tf_op jit(solution)/shard_map/ppermute | solution.py:24
  64.8 4.3 %collective-permute-done.21 = f32[2,64,256]{2,1,0:T(8,128)S(1)} collective-permute-done((f32[2,64,256]{2,1,0:T(8,128)S(1)}, f32[2,64,256]{2,1,0:T(8,128)S(1)}, u32[]{:S(2)}, u32[]{:S(2)}) %collective-permute-start.21) | collective-permute-done | bytes 131104 | tf_op jit(solution)/shard_map/ppermute | solution.py:24
  69.2 3.4 %collective-permute-start.24 = (f32[2,64,256]{2,1,0:T(8,128)S(1)}, f32[2,64,256]{2,1,0:T(8,128)S(1)}, u32[]{:S(2)}, u32[]{:S(2)}) collective-permute-start(f32[2,64,256]{2,1,0:T(8,128)S(1)} %add_add_fusion.1), channel_id=1, source_target_pairs={{0,32},{1,48},{2,34},{3,50},{4,36},{5,52},{6,38},{7,54},{8,40},{9,... | collective-permute-start | bytes 393224 | tf_op jit(solution)/shard_map/ppermute | solution.py:24
  72.6 1.3 %collective-permute-done.25 = f32[2,64,256]{2,1,0:T(8,128)S(1)} collective-permute-done((f32[2,64,256]{2,1,0:T(8,128)S(1)}, f32[2,64,256]{2,1,0:T(8,128)S(1)}, u32[]{:S(2)}, u32[]{:S(2)}) %collective-permute-start.25) | collective-permute-done | bytes 131104 | tf_op jit(solution)/shard_map/ppermute | solution.py:24
  73.9 3.0 %collective-permute-start.28 = (f32[2,64,256]{2,1,0:T(8,128)S(1)}, f32[2,64,256]{2,1,0:T(8,128)S(1)}, u32[]{:S(2)}, u32[]{:S(2)}) collective-permute-start(f32[2,64,256]{2,1,0:T(8,128)S(1)} %add_add_fusion), channel_id=1, source_target_pairs={{0,0},{1,16},{2,2},{3,18},{4,4},{5,20},{6,6},{7,22},{8,8},{9,24},{... | collective-permute-start | bytes 393224 | tf_op jit(solution)/shard_map/ppermute | solution.py:24
  77.1 3.1 %collective-permute-done.28.own_same = f32[2,64,256]{2,1,0:T(8,128)S(1)} collective-permute-done((f32[2,64,256]{2,1,0:T(8,128)S(1)}, f32[2,64,256]{2,1,0:T(8,128)S(1)}, u32[]{:S(2)}, u32[]{:S(2)}) %collective-permute-start.28) | collective-permute-done | bytes 131104 | tf_op jit(solution)/shard_map/ppermute | solution.py:24
  80.2 1.3 %collective-permute-done.30.got_same = f32[2,64,256]{2,1,0:T(8,128)S(1)} collective-permute-done((f32[2,64,256]{2,1,0:T(8,128)S(1)}, f32[2,64,256]{2,1,0:T(8,128)S(1)}, u32[]{:S(2)}, u32[]{:S(2)}) %collective-permute-start.30) | collective-permute-done | bytes 131104 | tf_op jit(solution)/shard_map/ppermute | solution.py:24
  81.6 1.5 %shard_map.44 = f32[256,2,256]{2,1,0:T(2,128)} custom-call(s32[2,16]{1,0:T(2,128)S(1)} %copy-done.3, f32[2,64,256]{2,1,0:T(8,128)S(1)} %collective-permute-done.24.own_flip, f32[2,64,256]{2,1,0:T(8,128)S(1)} %collective-permute-done.28.own_same, f32[2,64,256]{2,1,0:T(8,128)S(1)} %collective-permute-done.29.got_flip, ...), custom_call_target="tpu_custom_call" | custom-call | bytes 1048704 | tf_op jit(solution)/shard_map/pallas_call | solution.py:66
  (40 shorter events, 0.9 us)
Async XLA Ops:
  0.0 1.2 %copy-start = (f32[256,1024]{1,0:T(8,128)S(1)}, f32[256,1024]{1,0:T(8,128)}, u32[]{:S(2)}) copy-start(f32[256,1024]{1,0:T(8,128)} %inverse_ref.1) | copy-start | bytes 3145732
  1.2 0.7 copy-start.2
  1.9 4.0 %copy-start.1 = (f32[1024,2,64]{0,2,1:T(8,128)S(1)}, f32[1024,2,64]{0,2,1:T(8,128)}, u32[]{:S(2)}) copy-start(f32[1024,2,64]{0,2,1:T(8,128)} %param.4) | copy-start | bytes 1572868
  2.6 7.7 %collective-permute-start.2 = (f32[2,128,512]{2,1,0:T(8,128)S(1)}, f32[2,128,512]{2,1,0:T(8,128)S(1)}, u32[]{:S(2)}, u32[]{:S(2)}) collective-permute-start(f32[2,128,512]{2,1,0:T(8,128)S(1)} %get-tuple-element.36), channel_id=1, source_target_pairs={{0,1},{1,0},{2,3},{3,2},{4,5},{5,4},{6,7},{7,6},{8,9},{9,8},{10,11... | collective-permute-start | bytes 1572872 | tf_op jit(solution)/shard_map/ppermute | solution.py:24
  6.5 6.6 %collective-permute-start = (f32[64,512]{1,0:T(8,128)S(1)}, f32[64,512]{1,0:T(8,128)S(1)}, u32[]{:S(2)}, u32[]{:S(2)}) collective-permute-start(f32[64,512]{1,0:T(8,128)S(1)} %get-tuple-element.33), channel_id=1, source_target_pairs={{0,0},{1,16},{2,2},{3,18},{4,4},{5,20},{6,6},{7,22},{8,8},{9,24},{... | collective-permute-start | bytes 393224 | tf_op jit(solution)/shard_map/ppermute | solution.py:24
  8.4 6.7 %collective-permute-start.1 = (f32[64,512]{1,0:T(8,128)S(1)}, f32[64,512]{1,0:T(8,128)S(1)}, u32[]{:S(2)}, u32[]{:S(2)}) collective-permute-start(f32[64,512]{1,0:T(8,128)S(1)} %get-tuple-element.34), channel_id=1, source_target_pairs={{0,32},{1,48},{2,34},{3,50},{4,36},{5,52},{6,38},{7,54},{8,40},{9,... | collective-permute-start | bytes 393224 | tf_op jit(solution)/shard_map/ppermute | solution.py:24
  15.1 1.7 %collective-permute-start.3 = (f32[64,512]{1,0:T(8,128)S(1)}, f32[64,512]{1,0:T(8,128)S(1)}, u32[]{:S(2)}, u32[]{:S(2)}) collective-permute-start(f32[64,512]{1,0:T(8,128)S(1)} %collective-permute-done), channel_id=1, source_target_pairs={{0,1},{1,0},{2,3},{3,2},{4,5},{5,4},{6,7},{7,6},{8,9},{9,8},{10,11... | collective-permute-start | bytes 393224 | tf_op jit(solution)/shard_map/ppermute | solution.py:24
  15.3 1.5 %collective-permute-start.4 = (f32[64,512]{1,0:T(8,128)S(1)}, f32[64,512]{1,0:T(8,128)S(1)}, u32[]{:S(2)}, u32[]{:S(2)}) collective-permute-start(f32[64,512]{1,0:T(8,128)S(1)} %collective-permute-done.1), channel_id=1, source_target_pairs={{0,1},{1,0},{2,3},{3,2},{4,5},{5,4},{6,7},{7,6},{8,9},{9,8},{10,11... | collective-permute-start | bytes 393224 | tf_op jit(solution)/shard_map/ppermute | solution.py:24
  15.6 9.2 %collective-permute-start.7 = (f32[128,512]{1,0:T(8,128)S(1)}, f32[128,512]{1,0:T(8,128)S(1)}, u32[]{:S(2)}, u32[]{:S(2)}) collective-permute-start(f32[128,512]{1,0:T(8,128)S(1)} %get-tuple-element.42), channel_id=1, source_target_pairs={{0,32},{1,33},{2,34},{3,35},{4,36},{5,37},{6,38},{7,39},{8,40},{9,... | collective-permute-start | bytes 786440 | tf_op jit(solution)/shard_map/ppermute | solution.py:24
  16.8 9.0 %collective-permute-start.5 = (f32[2,64,512]{2,1,0:T(8,128)S(1)}, f32[2,64,512]{2,1,0:T(8,128)S(1)}, u32[]{:S(2)}, u32[]{:S(2)}) collective-permute-start(f32[2,64,512]{2,1,0:T(8,128)S(1)} %pad_maximum_fusion), channel_id=1, source_target_pairs={{0,2},{1,15},{2,4},{3,1},{4,6},{5,3},{6,8},{7,5},{8,10},{9,7},{10,... | collective-permute-start | bytes 786440 | tf_op jit(solution)/shard_map/ppermute | solution.py:24
  22.5 6.9 %collective-permute-start.6 = (f32[2,64,512]{2,1,0:T(8,128)S(1)}, f32[2,64,512]{2,1,0:T(8,128)S(1)}, u32[]{:S(2)}, u32[]{:S(2)}) collective-permute-start(f32[2,64,512]{2,1,0:T(8,128)S(1)} %pad_maximum_fusion.1), channel_id=1, source_target_pairs={{0,2},{1,15},{2,4},{3,1},{4,6},{5,3},{6,8},{7,5},{8,10},{9,7},{10,... | collective-permute-start | bytes 786440 | tf_op jit(solution)/shard_map/ppermute | solution.py:24
  23.2 9.7 %collective-permute-start.10 = (f32[128,512]{1,0:T(8,128)S(1)}, f32[128,512]{1,0:T(8,128)S(1)}, u32[]{:S(2)}, u32[]{:S(2)}) collective-permute-start(f32[128,512]{1,0:T(8,128)S(1)} %get-tuple-element.37.refs_0_), channel_id=1, source_target_pairs={{0,16},{1,17},{2,18},{3,19},{4,20},{5,21},{6,22},{7,23},{8,24},{9,... | collective-permute-start | bytes 786440 | tf_op jit(solution)/shard_map/ppermute | solution.py:24
  25.8 7.1 %collective-permute-start.8 = (f32[2,64,512]{2,1,0:T(8,128)S(1)}, f32[2,64,512]{2,1,0:T(8,128)S(1)}, u32[]{:S(2)}, u32[]{:S(2)}) collective-permute-start(f32[2,64,512]{2,1,0:T(8,128)S(1)} %collective-permute-done.5.refs_2_), channel_id=1, source_target_pairs={{0,2},{1,15},{2,4},{3,1},{4,6},{5,3},{6,8},{7,5},{8,10},{9,7},{10,... | collective-permute-start | bytes 786440 | tf_op jit(solution)/shard_map/ppermute | solution.py:24
  29.4 6.4 %collective-permute-start.9 = (f32[2,64,512]{2,1,0:T(8,128)S(1)}, f32[2,64,512]{2,1,0:T(8,128)S(1)}, u32[]{:S(2)}, u32[]{:S(2)}) collective-permute-start(f32[2,64,512]{2,1,0:T(8,128)S(1)} %collective-permute-done.6.refs_3_), channel_id=1, source_target_pairs={{0,2},{1,15},{2,4},{3,1},{4,6},{5,3},{6,8},{7,5},{8,10},{9,7},{10,... | collective-permute-start | bytes 786440 | tf_op jit(solution)/shard_map/ppermute | solution.py:24
  31.7 8.5 %collective-permute-start.13 = (f32[128,512]{1,0:T(8,128)S(1)}, f32[128,512]{1,0:T(8,128)S(1)}, u32[]{:S(2)}, u32[]{:S(2)}) collective-permute-start(f32[128,512]{1,0:T(8,128)S(1)} %get-tuple-element.42), channel_id=1, source_target_pairs={{0,48},{1,49},{2,50},{3,51},{4,52},{5,53},{6,54},{7,55},{8,56},{9,... | collective-permute-start | bytes 786440 | tf_op jit(solution)/shard_map/ppermute | solution.py:24
  32.9 7.3 %collective-permute-start.11 = (f32[2,64,512]{2,1,0:T(8,128)S(1)}, f32[2,64,512]{2,1,0:T(8,128)S(1)}, u32[]{:S(2)}, u32[]{:S(2)}) collective-permute-start(f32[2,64,512]{2,1,0:T(8,128)S(1)} %collective-permute-done.8.refs_4_), channel_id=1, source_target_pairs={{0,2},{1,15},{2,4},{3,1},{4,6},{5,3},{6,8},{7,5},{8,10},{9,7},{10,... | collective-permute-start | bytes 786440 | tf_op jit(solution)/shard_map/ppermute | solution.py:24
  35.8 6.4 %collective-permute-start.12 = (f32[2,64,512]{2,1,0:T(8,128)S(1)}, f32[2,64,512]{2,1,0:T(8,128)S(1)}, u32[]{:S(2)}, u32[]{:S(2)}) collective-permute-start(f32[2,64,512]{2,1,0:T(8,128)S(1)} %collective-permute-done.9.refs_5_), channel_id=1, source_target_pairs={{0,2},{1,15},{2,4},{3,1},{4,6},{5,3},{6,8},{7,5},{8,10},{9,7},{10,... | collective-permute-start | bytes 786440 | tf_op jit(solution)/shard_map/ppermute | solution.py:24
  38.9 7.5 %collective-permute-start.14 = (f32[128,512]{1,0:T(8,128)S(1)}, f32[128,512]{1,0:T(8,128)S(1)}, u32[]{:S(2)}, u32[]{:S(2)}) collective-permute-start(f32[128,512]{1,0:T(8,128)S(1)} %get-tuple-element.37.refs_0_), channel_id=1, source_target_pairs={{0,1},{1,0},{2,3},{3,2},{4,5},{5,4},{6,7},{7,6},{8,9},{9,8},{10,11... | collective-permute-start | bytes 786440 | tf_op jit(solution)/shard_map/ppermute | solution.py:24
  38.9 7.5 %collective-permute-start.15 = (f32[128,512]{1,0:T(8,128)S(1)}, f32[128,512]{1,0:T(8,128)S(1)}, u32[]{:S(2)}, u32[]{:S(2)}) collective-permute-start(f32[128,512]{1,0:T(8,128)S(1)} %collective-permute-done.7.refs_1_), channel_id=1, source_target_pairs={{0,1},{1,0},{2,3},{3,2},{4,5},{5,4},{6,7},{7,6},{8,9},{9,8},{10,11... | collective-permute-start | bytes 786440 | tf_op jit(solution)/shard_map/ppermute | solution.py:24
  40.2 6.3 %collective-permute-start.16 = (f32[128,512]{1,0:T(8,128)S(1)}, f32[128,512]{1,0:T(8,128)S(1)}, u32[]{:S(2)}, u32[]{:S(2)}) collective-permute-start(f32[128,512]{1,0:T(8,128)S(1)} %collective-permute-done.10.refs_2_), channel_id=1, source_target_pairs={{0,1},{1,0},{2,3},{3,2},{4,5},{5,4},{6,7},{7,6},{8,9},{9,8},{10,11... | collective-permute-start | bytes 786440 | tf_op jit(solution)/shard_map/ppermute | solution.py:24
  42.2 4.5 %collective-permute-start.17 = (f32[128,512]{1,0:T(8,128)S(1)}, f32[128,512]{1,0:T(8,128)S(1)}, u32[]{:S(2)}, u32[]{:S(2)}) collective-permute-start(f32[128,512]{1,0:T(8,128)S(1)} %collective-permute-done.13.refs_3_), channel_id=1, source_target_pairs={{0,1},{1,0},{2,3},{3,2},{4,5},{5,4},{6,7},{7,6},{8,9},{9,8},{10,11... | collective-permute-start | bytes 786440 | tf_op jit(solution)/shard_map/ppermute | solution.py:24
  45.6 5.8 %collective-permute-start.18 = (f32[2,64,512]{2,1,0:T(8,128)S(1)}, f32[2,64,512]{2,1,0:T(8,128)S(1)}, u32[]{:S(2)}, u32[]{:S(2)}) collective-permute-start(f32[2,64,512]{2,1,0:T(8,128)S(1)} %pad_maximum_fusion.2), channel_id=1, source_target_pairs={{0,2},{1,15},{2,4},{3,1},{4,6},{5,3},{6,8},{7,5},{8,10},{9,7},{10,... | collective-permute-start | bytes 786440 | tf_op jit(solution)/shard_map/ppermute | solution.py:24
  51.4 4.1 %collective-permute-start.19 = (f32[7,64,256]{2,1,0:T(8,128)S(1)}, f32[7,64,256]{2,1,0:T(8,128)S(1)}, u32[]{:S(2)}, u32[]{:S(2)}) collective-permute-start(f32[7,64,256]{2,1,0:T(8,128)S(1)} %get-tuple-element.51), channel_id=1, source_target_pairs={{0,1},{1,0},{2,3},{3,2},{4,5},{5,4},{6,7},{7,6},{8,9},{9,8},{10,11... | collective-permute-start | bytes 1376264 | tf_op jit(solution)/shard_map/ppermute | solution.py:24
  54.1 1.3 %collective-permute-start.20 = (f32[1,64,256]{2,1,0:T(8,128)S(1)}, f32[1,64,256]{2,1,0:T(8,128)S(1)}, u32[]{:S(2)}, u32[]{:S(2)}) collective-permute-start(f32[1,64,256]{2,1,0:T(8,128)S(1)} %get-tuple-element.52), channel_id=1, source_target_pairs={{0,1},{1,0},{2,3},{3,2},{4,5},{5,4},{6,7},{7,6},{8,9},{9,8},{10,11... | collective-permute-start | bytes 196616 | tf_op jit(solution)/shard_map/ppermute | solution.py:24
  56.1 7.7 %collective-permute-start.23 = (f32[2,64,256]{2,1,0:T(8,128)S(1)}, f32[2,64,256]{2,1,0:T(8,128)S(1)}, u32[]{:S(2)}, u32[]{:S(2)}) collective-permute-start(f32[2,64,256]{2,1,0:T(8,128)S(1)} %get-tuple-element.56), channel_id=1, source_target_pairs={{0,192},{1,193},{2,194},{3,195},{4,196},{5,197},{6,198},{7,199},{8... | collective-permute-start | bytes 393224 | tf_op jit(solution)/shard_map/ppermute | solution.py:24
  58.6 6.2 %collective-permute-start.22 = (f32[2,64,256]{2,1,0:T(8,128)S(1)}, f32[2,64,256]{2,1,0:T(8,128)S(1)}, u32[]{:S(2)}, u32[]{:S(2)}) collective-permute-start(f32[2,64,256]{2,1,0:T(8,128)S(1)} %get-tuple-element.55), channel_id=1, source_target_pairs={{0,128},{1,129},{2,130},{3,131},{4,132},{5,133},{6,134},{7,135},{8... | collective-permute-start | bytes 393224 | tf_op jit(solution)/shard_map/ppermute | solution.py:24
  59.2 10.0 %collective-permute-start.21 = (f32[2,64,256]{2,1,0:T(8,128)S(1)}, f32[2,64,256]{2,1,0:T(8,128)S(1)}, u32[]{:S(2)}, u32[]{:S(2)}) collective-permute-start(f32[2,64,256]{2,1,0:T(8,128)S(1)} %get-tuple-element.54), channel_id=1, source_target_pairs={{0,64},{1,65},{2,66},{3,67},{4,68},{5,69},{6,70},{7,71},{8,72},{9,... | collective-permute-start | bytes 393224 | tf_op jit(solution)/shard_map/ppermute | solution.py:24
  59.8 12.8 %collective-permute-start.27 = (f32[2,64,256]{2,1,0:T(8,128)S(1)}, f32[2,64,256]{2,1,0:T(8,128)S(1)}, u32[]{:S(2)}, u32[]{:S(2)}) collective-permute-start(f32[2,64,256]{2,1,0:T(8,128)S(1)} %get-tuple-element.60), channel_id=1, source_target_pairs={{0,192},{1,193},{2,194},{3,195},{4,196},{5,197},{6,198},{7,199},{8... | collective-permute-start | bytes 393224 | tf_op jit(solution)/shard_map/ppermute | solution.py:24
  61.8 10.8 %collective-permute-start.26 = (f32[2,64,256]{2,1,0:T(8,128)S(1)}, f32[2,64,256]{2,1,0:T(8,128)S(1)}, u32[]{:S(2)}, u32[]{:S(2)}) collective-permute-start(f32[2,64,256]{2,1,0:T(8,128)S(1)} %get-tuple-element.59), channel_id=1, source_target_pairs={{0,128},{1,129},{2,130},{3,131},{4,132},{5,133},{6,134},{7,135},{8... | collective-permute-start | bytes 393224 | tf_op jit(solution)/shard_map/ppermute | solution.py:24
  63.8 10.1 %collective-permute-start.25 = (f32[2,64,256]{2,1,0:T(8,128)S(1)}, f32[2,64,256]{2,1,0:T(8,128)S(1)}, u32[]{:S(2)}, u32[]{:S(2)}) collective-permute-start(f32[2,64,256]{2,1,0:T(8,128)S(1)} %get-tuple-element.58), channel_id=1, source_target_pairs={{0,64},{1,65},{2,66},{3,67},{4,68},{5,69},{6,70},{7,71},{8,72},{9,... | collective-permute-start | bytes 393224 | tf_op jit(solution)/shard_map/ppermute | solution.py:24
  69.2 7.8 %collective-permute-start.24 = (f32[2,64,256]{2,1,0:T(8,128)S(1)}, f32[2,64,256]{2,1,0:T(8,128)S(1)}, u32[]{:S(2)}, u32[]{:S(2)}) collective-permute-start(f32[2,64,256]{2,1,0:T(8,128)S(1)} %add_add_fusion.1), channel_id=1, source_target_pairs={{0,32},{1,48},{2,34},{3,50},{4,36},{5,52},{6,38},{7,54},{8,40},{9,... | collective-permute-start | bytes 393224 | tf_op jit(solution)/shard_map/ppermute | solution.py:24
  73.9 7.7 %copy-start.3 = (s32[2,16]{1,0:T(2,128)S(1)}, s32[2,16]{1,0:T(2,128)}, u32[]{:S(2)}) copy-start(s32[2,16]{1,0:T(2,128)} %pattern_ref.7) | copy-start | bytes 388
  73.9 6.3 %collective-permute-start.28 = (f32[2,64,256]{2,1,0:T(8,128)S(1)}, f32[2,64,256]{2,1,0:T(8,128)S(1)}, u32[]{:S(2)}, u32[]{:S(2)}) collective-permute-start(f32[2,64,256]{2,1,0:T(8,128)S(1)} %add_add_fusion), channel_id=1, source_target_pairs={{0,0},{1,16},{2,2},{3,18},{4,4},{5,20},{6,6},{7,22},{8,8},{9,24},{... | collective-permute-start | bytes 393224 | tf_op jit(solution)/shard_map/ppermute | solution.py:24
  77.0 3.2 %collective-permute-start.29 = (f32[2,64,256]{2,1,0:T(8,128)S(1)}, f32[2,64,256]{2,1,0:T(8,128)S(1)}, u32[]{:S(2)}, u32[]{:S(2)}) collective-permute-start(f32[2,64,256]{2,1,0:T(8,128)S(1)} %collective-permute-done.24.own_flip), channel_id=1, source_target_pairs={{0,1},{1,0},{2,3},{3,2},{4,5},{5,4},{6,7},{7,6},{8,9},{9,8},{10,11... | collective-permute-start | bytes 393224 | tf_op jit(solution)/shard_map/ppermute | solution.py:24
  80.2 1.3 %collective-permute-start.30 = (f32[2,64,256]{2,1,0:T(8,128)S(1)}, f32[2,64,256]{2,1,0:T(8,128)S(1)}, u32[]{:S(2)}, u32[]{:S(2)}) collective-permute-start(f32[2,64,256]{2,1,0:T(8,128)S(1)} %collective-permute-done.28.own_same), channel_id=1, source_target_pairs={{0,1},{1,0},{2,3},{3,2},{4,5},{5,4},{6,7},{7,6},{8,9},{9,8},{10,11... | collective-permute-start | bytes 393224 | tf_op jit(solution)/shard_map/ppermute | solution.py:24

commit v3 on v2

--- a/solution.py
+++ b/solution.py
@@ -235,13 +235,13 @@
     early = [pairs[0][:1], pairs[1][:1]]
     for step in range(3):
         if step:
-            pairs[0] = after(pairs[0], blocks[step])
+            pairs[0] = after(pairs[0], blocks[step + 1])
         pairs = [send(part, ring) for part in pairs]
         early += pairs
     last = send(jnp.concatenate([part[:1] for part in pairs]), ring)
     late = [last[:1], last[1:]]
 
-    blocks[3] = after(blocks[3], *pairs)
+    blocks[1] = after(blocks[1], *pairs)
     halves = [send(block, other_core) for block in blocks]
     whole = ((4 * B, 2 * B), BF16)
     a_high, a_low = call(split_inverse, [whole, whole], *blocks, *halves)

time: 83.3 us -> 81.7 us (0.981)
  starting transfers between devices: 48.8 us -> 47.2 us
    ppermute x31, starting transfers between devices: 48.8 us -> 47.2 us  [send(): return lax.ppermute(array, AXES, pairs)]
  transfers between devices with their start and end apart: 31 -> 31, of which waited for: 15 -> 16; matrix products, arithmetic and copies ran while one was open for 0% -> 0% of each run, Pallas kernels for 5% -> 5%
where the time goes in v3:
time: 81.7 us; the launch traced here: 81.5 us
  starting transfers between devices  47.2 us (58%)
  waiting for transfers between devices  25.2 us (31%)
  Pallas kernels  6.84 us (8%)
  local copies, waits for them, and re-layouts  1.97 us (2%)
    ppermute x31, starting transfers between devices, send(): return lax.ppermute(array, AXES, pairs)  47.2 us
    ppermute x31, waiting for transfers between devices, send(): return lax.ppermute(array, AXES, pairs)  25.2 us
    pallas_call x8, Pallas kernels, call(): pl.pallas_call(kernel, out_shape=shapes, in_specs=in_specs, out_specs=[pl...  6.84 us
    unnamed x8, local copies, waits for them, and re-layouts  1.91 us
  transfers between devices with their start and end apart: 31, of which 16 were waited for; matrix products, arithmetic and copies ran while one was open for 0% of the time, Pallas kernels for 5%

profile of v3, /device:TPU:1, one launch (start us, length us, event | category | flops | bytes accessed | tf_op | source)
XLA Modules:
  0.0 81.5 jit_solution(15145260970859549444)
XLA Ops:
  0.0 1.2 %copy-done = f32[256,1024]{1,0:T(8,128)S(1)} copy-done((f32[256,1024]{1,0:T(8,128)S(1)}, f32[256,1024]{1,0:T(8,128)}, u32[]{:S(2)}) %copy-start) | copy-done | bytes 1048600
  1.2 0.7 copy-done.2
  1.9 0.6 shard_map.38
  2.6 3.3 %collective-permute-start.2 = (f32[2,128,512]{2,1,0:T(8,128)S(1)}, f32[2,128,512]{2,1,0:T(8,128)S(1)}, u32[]{:S(2)}, u32[]{:S(2)}) collective-permute-start(f32[2,128,512]{2,1,0:T(8,128)S(1)} %get-tuple-element.36), channel_id=1, source_target_pairs={{0,1},{1,0},{2,3},{3,2},{4,5},{5,4},{6,7},{7,6},{8,9},{9,8},{10,11... | collective-permute-start | bytes 1572872 | tf_op jit(solution)/shard_map/ppermute | solution.py:24
  5.9 0.6 shard_map.37
  6.5 1.9 %collective-permute-start = (f32[64,512]{1,0:T(8,128)S(1)}, f32[64,512]{1,0:T(8,128)S(1)}, u32[]{:S(2)}, u32[]{:S(2)}) collective-permute-start(f32[64,512]{1,0:T(8,128)S(1)} %get-tuple-element.33), channel_id=1, source_target_pairs={{0,0},{1,16},{2,2},{3,18},{4,4},{5,20},{6,6},{7,22},{8,8},{9,24},{... | collective-permute-start | bytes 393224 | tf_op jit(solution)/shard_map/ppermute | solution.py:24
  8.4 1.8 %collective-permute-start.1 = (f32[64,512]{1,0:T(8,128)S(1)}, f32[64,512]{1,0:T(8,128)S(1)}, u32[]{:S(2)}, u32[]{:S(2)}) collective-permute-start(f32[64,512]{1,0:T(8,128)S(1)} %get-tuple-element.34), channel_id=1, source_target_pairs={{0,32},{1,48},{2,34},{3,50},{4,36},{5,52},{6,38},{7,54},{8,40},{9,... | collective-permute-start | bytes 393224 | tf_op jit(solution)/shard_map/ppermute | solution.py:24
  10.2 0.6 shard_map.39
  10.9 2.2 %collective-permute-done = f32[64,512]{1,0:T(8,128)S(1)} collective-permute-done((f32[64,512]{1,0:T(8,128)S(1)}, f32[64,512]{1,0:T(8,128)S(1)}, u32[]{:S(2)}, u32[]{:S(2)}) %collective-permute-start) | collective-permute-done | bytes 131104 | tf_op jit(solution)/shard_map/ppermute | solution.py:24
  13.1 2.1 %collective-permute-done.1 = f32[64,512]{1,0:T(8,128)S(1)} collective-permute-done((f32[64,512]{1,0:T(8,128)S(1)}, f32[64,512]{1,0:T(8,128)S(1)}, u32[]{:S(2)}, u32[]{:S(2)}) %collective-permute-start.1) | collective-permute-done | bytes 131104 | tf_op jit(solution)/shard_map/ppermute | solution.py:24
  15.1 0.2 collective-permute-start.3
  15.3 0.3 collective-permute-start.4
  15.6 0.8 %collective-permute-done.3 = f32[64,512]{1,0:T(8,128)S(1)} collective-permute-done((f32[64,512]{1,0:T(8,128)S(1)}, f32[64,512]{1,0:T(8,128)S(1)}, u32[]{:S(2)}, u32[]{:S(2)}) %collective-permute-start.3) | collective-permute-done | bytes 131104 | tf_op jit(solution)/shard_map/ppermute | solution.py:24
  16.7 4.4 %collective-permute-start.5 = (f32[2,64,512]{2,1,0:T(8,128)S(1)}, f32[2,64,512]{2,1,0:T(8,128)S(1)}, u32[]{:S(2)}, u32[]{:S(2)}) collective-permute-start(f32[2,64,512]{2,1,0:T(8,128)S(1)} %pad_maximum_fusion), channel_id=1, source_target_pairs={{0,2},{1,15},{2,4},{3,1},{4,6},{5,3},{6,8},{7,5},{8,10},{9,7},{10,... | collective-permute-start | bytes 786440 | tf_op jit(solution)/shard_map/ppermute | solution.py:24
  21.0 0.7 collective-permute-start.6
  21.8 2.5 %collective-permute-start.10 = (f32[128,512]{1,0:T(8,128)S(1)}, f32[128,512]{1,0:T(8,128)S(1)}, u32[]{:S(2)}, u32[]{:S(2)}) collective-permute-start(f32[128,512]{1,0:T(8,128)S(1)} %get-tuple-element.43), channel_id=1, source_target_pairs={{0,48},{1,49},{2,50},{3,51},{4,52},{5,53},{6,54},{7,55},{8,56},{9,... | collective-permute-start | bytes 786440 | tf_op jit(solution)/shard_map/ppermute | solution.py:24
  24.4 3.5 %collective-permute-start.8 = (f32[2,64,512]{2,1,0:T(8,128)S(1)}, f32[2,64,512]{2,1,0:T(8,128)S(1)}, u32[]{:S(2)}, u32[]{:S(2)}) collective-permute-start(f32[2,64,512]{2,1,0:T(8,128)S(1)} %collective-permute-done.5.refs_2_), channel_id=1, source_target_pairs={{0,2},{1,15},{2,4},{3,1},{4,6},{5,3},{6,8},{7,5},{8,10},{9,7},{10,... | collective-permute-start | bytes 786440 | tf_op jit(solution)/shard_map/ppermute | solution.py:24
  27.9 2.7 %collective-permute-start.9 = (f32[2,64,512]{2,1,0:T(8,128)S(1)}, f32[2,64,512]{2,1,0:T(8,128)S(1)}, u32[]{:S(2)}, u32[]{:S(2)}) collective-permute-start(f32[2,64,512]{2,1,0:T(8,128)S(1)} %collective-permute-done.6.refs_3_), channel_id=1, source_target_pairs={{0,2},{1,15},{2,4},{3,1},{4,6},{5,3},{6,8},{7,5},{8,10},{9,7},{10,... | collective-permute-start | bytes 786440 | tf_op jit(solution)/shard_map/ppermute | solution.py:24
  30.6 2.1 %collective-permute-start.13 = (f32[128,512]{1,0:T(8,128)S(1)}, f32[128,512]{1,0:T(8,128)S(1)}, u32[]{:S(2)}, u32[]{:S(2)}) collective-permute-start(f32[128,512]{1,0:T(8,128)S(1)} %get-tuple-element.43), channel_id=1, source_target_pairs={{0,32},{1,33},{2,34},{3,35},{4,36},{5,37},{6,38},{7,39},{8,40},{9,... | collective-permute-start | bytes 786440 | tf_op jit(solution)/shard_map/ppermute | solution.py:24
  32.7 1.6 %collective-permute-start.11 = (f32[2,64,512]{2,1,0:T(8,128)S(1)}, f32[2,64,512]{2,1,0:T(8,128)S(1)}, u32[]{:S(2)}, u32[]{:S(2)}) collective-permute-start(f32[2,64,512]{2,1,0:T(8,128)S(1)} %collective-permute-done.8.refs_4_), channel_id=1, source_target_pairs={{0,2},{1,15},{2,4},{3,1},{4,6},{5,3},{6,8},{7,5},{8,10},{9,7},{10,... | collective-permute-start | bytes 786440 | tf_op jit(solution)/shard_map/ppermute | solution.py:24
  34.3 3.1 %collective-permute-start.12 = (f32[2,64,512]{2,1,0:T(8,128)S(1)}, f32[2,64,512]{2,1,0:T(8,128)S(1)}, u32[]{:S(2)}, u32[]{:S(2)}) collective-permute-start(f32[2,64,512]{2,1,0:T(8,128)S(1)} %collective-permute-done.9.refs_5_), channel_id=1, source_target_pairs={{0,2},{1,15},{2,4},{3,1},{4,6},{5,3},{6,8},{7,5},{8,10},{9,7},{10,... | collective-permute-start | bytes 786440 | tf_op jit(solution)/shard_map/ppermute | solution.py:24
  37.4 0.5 collective-permute-start.16
  37.9 0.9 %collective-permute-done.13.refs_1_ = f32[128,512]{1,0:T(8,128)S(1)} collective-permute-done((f32[128,512]{1,0:T(8,128)S(1)}, f32[128,512]{1,0:T(8,128)S(1)}, u32[]{:S(2)}, u32[]{:S(2)}) %collective-permute-start.13) | collective-permute-done | bytes 262176 | tf_op jit(solution)/shard_map/ppermute | solution.py:24
  38.8 2.2 %collective-permute-done.12.refs_7_ = f32[2,64,512]{2,1,0:T(8,128)S(1)} collective-permute-done((f32[2,64,512]{2,1,0:T(8,128)S(1)}, f32[2,64,512]{2,1,0:T(8,128)S(1)}, u32[]{:S(2)}, u32[]{:S(2)}) %collective-permute-start.12) | collective-permute-done | bytes 262176 | tf_op jit(solution)/shard_map/ppermute | solution.py:24
  41.0 2.9 %collective-permute-start.15 = (f32[128,512]{1,0:T(8,128)S(1)}, f32[128,512]{1,0:T(8,128)S(1)}, u32[]{:S(2)}, u32[]{:S(2)}) collective-permute-start(f32[128,512]{1,0:T(8,128)S(1)} %collective-permute-done.13.refs_1_), channel_id=1, source_target_pairs={{0,1},{1,0},{2,3},{3,2},{4,5},{5,4},{6,7},{7,6},{8,9},{9,8},{10,11... | collective-permute-start | bytes 786440 | tf_op jit(solution)/shard_map/ppermute | solution.py:24
  44.0 0.5 collective-permute-start.18
  44.6 0.6 collective-permute-done.15.refs_5_
  45.1 0.6 shard_map.40
  45.8 1.6 %shard_map.41 = (f32[7,64,256]{2,1,0:T(8,128)S(1)}, f32[7,64,256]{2,1,0:T(8,128)S(1)}) custom-call(f32[1,64,512]{2,1,0:T(8,128)S(1)} %slice.18.refs_0_, f32[1,64,512]{2,1,0:T(8,128)S(1)} %slice.19.refs_1_, f32[2,64,512]{2,1,0:T(8,128)S(1)} %collective-permute-done.5.refs_2_, f32[2,64,512]{2,1,0:T(8,128)S(1)} %collective-permute-done.6.refs_3_, ...), custom_call_target="tpu_custom_call" | custom-call | flops 1409286144 | bytes 4849664 | tf_op jit(solution)/shard_map/pallas_call | solution.py:66
  47.4 2.5 %collective-permute-done.18 = f32[2,64,512]{2,1,0:T(8,128)S(1)} collective-permute-done((f32[2,64,512]{2,1,0:T(8,128)S(1)}, f32[2,64,512]{2,1,0:T(8,128)S(1)}, u32[]{:S(2)}, u32[]{:S(2)}) %collective-permute-start.18) | collective-permute-done | bytes 262176 | tf_op jit(solution)/shard_map/ppermute | solution.py:24
  49.8 2.1 %collective-permute-start.19 = (f32[7,64,256]{2,1,0:T(8,128)S(1)}, f32[7,64,256]{2,1,0:T(8,128)S(1)}, u32[]{:S(2)}, u32[]{:S(2)}) collective-permute-start(f32[7,64,256]{2,1,0:T(8,128)S(1)} %get-tuple-element.51), channel_id=1, source_target_pairs={{0,1},{1,0},{2,3},{3,2},{4,5},{5,4},{6,7},{7,6},{8,9},{9,8},{10,11... | collective-permute-start | bytes 1376264 | tf_op jit(solution)/shard_map/ppermute | solution.py:24
  51.9 0.6 shard_map.42
  52.7 1.2 %collective-permute-done.20.got_late = f32[1,64,256]{2,1,0:T(8,128)S(1)} collective-permute-done((f32[1,64,256]{2,1,0:T(8,128)S(1)}, f32[1,64,256]{2,1,0:T(8,128)S(1)}, u32[]{:S(2)}, u32[]{:S(2)}) %collective-permute-start.20) | collective-permute-done | bytes 65568 | tf_op jit(solution)/shard_map/ppermute | solution.py:24
  53.9 0.6 shard_map.43
  54.5 2.5 %collective-permute-start.23 = (f32[2,64,256]{2,1,0:T(8,128)S(1)}, f32[2,64,256]{2,1,0:T(8,128)S(1)}, u32[]{:S(2)}, u32[]{:S(2)}) collective-permute-start(f32[2,64,256]{2,1,0:T(8,128)S(1)} %get-tuple-element.56), channel_id=1, source_target_pairs={{0,192},{1,193},{2,194},{3,195},{4,196},{5,197},{6,198},{7,199},{8... | collective-permute-start | bytes 393224 | tf_op jit(solution)/shard_map/ppermute | solution.py:24
  57.1 0.5 collective-permute-start.22
  57.6 0.6 collective-permute-start.21
  58.2 2.1 %collective-permute-start.27 = (f32[2,64,256]{2,1,0:T(8,128)S(1)}, f32[2,64,256]{2,1,0:T(8,128)S(1)}, u32[]{:S(2)}, u32[]{:S(2)}) collective-permute-start(f32[2,64,256]{2,1,0:T(8,128)S(1)} %get-tuple-element.60), channel_id=1, source_target_pairs={{0,192},{1,193},{2,194},{3,195},{4,196},{5,197},{6,198},{7,199},{8... | collective-permute-start | bytes 393224 | tf_op jit(solution)/shard_map/ppermute | solution.py:24
  60.3 1.2 %collective-permute-start.26 = (f32[2,64,256]{2,1,0:T(8,128)S(1)}, f32[2,64,256]{2,1,0:T(8,128)S(1)}, u32[]{:S(2)}, u32[]{:S(2)}) collective-permute-start(f32[2,64,256]{2,1,0:T(8,128)S(1)} %get-tuple-element.59), channel_id=1, source_target_pairs={{0,128},{1,129},{2,130},{3,131},{4,132},{5,133},{6,134},{7,135},{8... | collective-permute-start | bytes 393224 | tf_op jit(solution)/shard_map/ppermute | solution.py:24
  61.5 0.8 collective-permute-done.23
  62.3 1.0 %collective-permute-done.22 = f32[2,64,256]{2,1,0:T(8,128)S(1)} collective-permute-done((f32[2,64,256]{2,1,0:T(8,128)S(1)}, f32[2,64,256]{2,1,0:T(8,128)S(1)}, u32[]{:S(2)}, u32[]{:S(2)}) %collective-permute-start.22) | collective-permute-done | bytes 131104 | tf_op jit(solution)/shard_map/ppermute | solution.py:24
  63.2 4.3 %collective-permute-done.21 = f32[2,64,256]{2,1,0:T(8,128)S(1)} collective-permute-done((f32[2,64,256]{2,1,0:T(8,128)S(1)}, f32[2,64,256]{2,1,0:T(8,128)S(1)}, u32[]{:S(2)}, u32[]{:S(2)}) %collective-permute-start.21) | collective-permute-done | bytes 131104 | tf_op jit(solution)/shard_map/ppermute | solution.py:24
  67.6 3.0 %collective-permute-start.24 = (f32[2,64,256]{2,1,0:T(8,128)S(1)}, f32[2,64,256]{2,1,0:T(8,128)S(1)}, u32[]{:S(2)}, u32[]{:S(2)}) collective-permute-start(f32[2,64,256]{2,1,0:T(8,128)S(1)} %add_add_fusion.1), channel_id=1, source_target_pairs={{0,32},{1,48},{2,34},{3,50},{4,36},{5,52},{6,38},{7,54},{8,40},{9,... | collective-permute-start | bytes 393224 | tf_op jit(solution)/shard_map/ppermute | solution.py:24
  70.6 1.7 %collective-permute-done.25 = f32[2,64,256]{2,1,0:T(8,128)S(1)} collective-permute-done((f32[2,64,256]{2,1,0:T(8,128)S(1)}, f32[2,64,256]{2,1,0:T(8,128)S(1)}, u32[]{:S(2)}, u32[]{:S(2)}) %collective-permute-start.25) | collective-permute-done | bytes 131104 | tf_op jit(solution)/shard_map/ppermute | solution.py:24
  72.3 2.8 %collective-permute-start.28 = (f32[2,64,256]{2,1,0:T(8,128)S(1)}, f32[2,64,256]{2,1,0:T(8,128)S(1)}, u32[]{:S(2)}, u32[]{:S(2)}) collective-permute-start(f32[2,64,256]{2,1,0:T(8,128)S(1)} %add_add_fusion), channel_id=1, source_target_pairs={{0,0},{1,16},{2,2},{3,18},{4,4},{5,20},{6,6},{7,22},{8,8},{9,24},{... | collective-permute-start | bytes 393224 | tf_op jit(solution)/shard_map/ppermute | solution.py:24
  75.3 3.3 %collective-permute-done.28.own_same = f32[2,64,256]{2,1,0:T(8,128)S(1)} collective-permute-done((f32[2,64,256]{2,1,0:T(8,128)S(1)}, f32[2,64,256]{2,1,0:T(8,128)S(1)}, u32[]{:S(2)}, u32[]{:S(2)}) %collective-permute-start.28) | collective-permute-done | bytes 131104 | tf_op jit(solution)/shard_map/ppermute | solution.py:24
  78.6 1.3 %collective-permute-done.30.got_same = f32[2,64,256]{2,1,0:T(8,128)S(1)} collective-permute-done((f32[2,64,256]{2,1,0:T(8,128)S(1)}, f32[2,64,256]{2,1,0:T(8,128)S(1)}, u32[]{:S(2)}, u32[]{:S(2)}) %collective-permute-start.30) | collective-permute-done | bytes 131104 | tf_op jit(solution)/shard_map/ppermute | solution.py:24
  80.0 1.5 %shard_map.44 = f32[256,2,256]{2,1,0:T(2,128)} custom-call(s32[2,16]{1,0:T(2,128)S(1)} %copy-done.3, f32[2,64,256]{2,1,0:T(8,128)S(1)} %collective-permute-done.24.own_flip, f32[2,64,256]{2,1,0:T(8,128)S(1)} %collective-permute-done.28.own_same, f32[2,64,256]{2,1,0:T(8,128)S(1)} %collective-permute-done.29.got_flip, ...), custom_call_target="tpu_custom_call" | custom-call | bytes 1048704 | tf_op jit(solution)/shard_map/pallas_call | solution.py:66
  (40 shorter events, 0.7 us)
Async XLA Ops:
  0.0 1.2 %copy-start = (f32[256,1024]{1,0:T(8,128)S(1)}, f32[256,1024]{1,0:T(8,128)}, u32[]{:S(2)}) copy-start(f32[256,1024]{1,0:T(8,128)} %inverse_ref.1) | copy-start | bytes 3145732
  1.2 0.7 copy-start.2
  1.9 4.0 %copy-start.1 = (f32[1024,2,64]{0,2,1:T(8,128)S(1)}, f32[1024,2,64]{0,2,1:T(8,128)}, u32[]{:S(2)}) copy-start(f32[1024,2,64]{0,2,1:T(8,128)} %param.4) | copy-start | bytes 1572868
  2.6 7.7 %collective-permute-start.2 = (f32[2,128,512]{2,1,0:T(8,128)S(1)}, f32[2,128,512]{2,1,0:T(8,128)S(1)}, u32[]{:S(2)}, u32[]{:S(2)}) collective-permute-start(f32[2,128,512]{2,1,0:T(8,128)S(1)} %get-tuple-element.36), channel_id=1, source_target_pairs={{0,1},{1,0},{2,3},{3,2},{4,5},{5,4},{6,7},{7,6},{8,9},{9,8},{10,11... | collective-permute-start | bytes 1572872 | tf_op jit(solution)/shard_map/ppermute | solution.py:24
  6.5 6.6 %collective-permute-start = (f32[64,512]{1,0:T(8,128)S(1)}, f32[64,512]{1,0:T(8,128)S(1)}, u32[]{:S(2)}, u32[]{:S(2)}) collective-permute-start(f32[64,512]{1,0:T(8,128)S(1)} %get-tuple-element.33), channel_id=1, source_target_pairs={{0,0},{1,16},{2,2},{3,18},{4,4},{5,20},{6,6},{7,22},{8,8},{9,24},{... | collective-permute-start | bytes 393224 | tf_op jit(solution)/shard_map/ppermute | solution.py:24
  8.4 6.7 %collective-permute-start.1 = (f32[64,512]{1,0:T(8,128)S(1)}, f32[64,512]{1,0:T(8,128)S(1)}, u32[]{:S(2)}, u32[]{:S(2)}) collective-permute-start(f32[64,512]{1,0:T(8,128)S(1)} %get-tuple-element.34), channel_id=1, source_target_pairs={{0,32},{1,48},{2,34},{3,50},{4,36},{5,52},{6,38},{7,54},{8,40},{9,... | collective-permute-start | bytes 393224 | tf_op jit(solution)/shard_map/ppermute | solution.py:24
  15.1 1.3 %collective-permute-start.3 = (f32[64,512]{1,0:T(8,128)S(1)}, f32[64,512]{1,0:T(8,128)S(1)}, u32[]{:S(2)}, u32[]{:S(2)}) collective-permute-start(f32[64,512]{1,0:T(8,128)S(1)} %collective-permute-done), channel_id=1, source_target_pairs={{0,1},{1,0},{2,3},{3,2},{4,5},{5,4},{6,7},{7,6},{8,9},{9,8},{10,11... | collective-permute-start | bytes 393224 | tf_op jit(solution)/shard_map/ppermute | solution.py:24
  15.3 1.4 %collective-permute-start.4 = (f32[64,512]{1,0:T(8,128)S(1)}, f32[64,512]{1,0:T(8,128)S(1)}, u32[]{:S(2)}, u32[]{:S(2)}) collective-permute-start(f32[64,512]{1,0:T(8,128)S(1)} %collective-permute-done.1), channel_id=1, source_target_pairs={{0,1},{1,0},{2,3},{3,2},{4,5},{5,4},{6,7},{7,6},{8,9},{9,8},{10,11... | collective-permute-start | bytes 393224 | tf_op jit(solution)/shard_map/ppermute | solution.py:24
  15.6 8.6 %collective-permute-start.7 = (f32[128,512]{1,0:T(8,128)S(1)}, f32[128,512]{1,0:T(8,128)S(1)}, u32[]{:S(2)}, u32[]{:S(2)}) collective-permute-start(f32[128,512]{1,0:T(8,128)S(1)} %get-tuple-element.37.refs_0_), channel_id=1, source_target_pairs={{0,16},{1,17},{2,18},{3,19},{4,20},{5,21},{6,22},{7,23},{8,24},{9,... | collective-permute-start | bytes 786440 | tf_op jit(solution)/shard_map/ppermute | solution.py:24
  16.7 7.7 %collective-permute-start.5 = (f32[2,64,512]{2,1,0:T(8,128)S(1)}, f32[2,64,512]{2,1,0:T(8,128)S(1)}, u32[]{:S(2)}, u32[]{:S(2)}) collective-permute-start(f32[2,64,512]{2,1,0:T(8,128)S(1)} %pad_maximum_fusion), channel_id=1, source_target_pairs={{0,2},{1,15},{2,4},{3,1},{4,6},{5,3},{6,8},{7,5},{8,10},{9,7},{10,... | collective-permute-start | bytes 786440 | tf_op jit(solution)/shard_map/ppermute | solution.py:24
  21.0 6.8 %collective-permute-start.6 = (f32[2,64,512]{2,1,0:T(8,128)S(1)}, f32[2,64,512]{2,1,0:T(8,128)S(1)}, u32[]{:S(2)}, u32[]{:S(2)}) collective-permute-start(f32[2,64,512]{2,1,0:T(8,128)S(1)} %pad_maximum_fusion.1), channel_id=1, source_target_pairs={{0,2},{1,15},{2,4},{3,1},{4,6},{5,3},{6,8},{7,5},{8,10},{9,7},{10,... | collective-permute-start | bytes 786440 | tf_op jit(solution)/shard_map/ppermute | solution.py:24
  21.8 10.9 %collective-permute-start.10 = (f32[128,512]{1,0:T(8,128)S(1)}, f32[128,512]{1,0:T(8,128)S(1)}, u32[]{:S(2)}, u32[]{:S(2)}) collective-permute-start(f32[128,512]{1,0:T(8,128)S(1)} %get-tuple-element.43), channel_id=1, source_target_pairs={{0,48},{1,49},{2,50},{3,51},{4,52},{5,53},{6,54},{7,55},{8,56},{9,... | collective-permute-start | bytes 786440 | tf_op jit(solution)/shard_map/ppermute | solution.py:24
  24.4 8.4 %collective-permute-start.8 = (f32[2,64,512]{2,1,0:T(8,128)S(1)}, f32[2,64,512]{2,1,0:T(8,128)S(1)}, u32[]{:S(2)}, u32[]{:S(2)}) collective-permute-start(f32[2,64,512]{2,1,0:T(8,128)S(1)} %collective-permute-done.5.refs_2_), channel_id=1, source_target_pairs={{0,2},{1,15},{2,4},{3,1},{4,6},{5,3},{6,8},{7,5},{8,10},{9,7},{10,... | collective-permute-start | bytes 786440 | tf_op jit(solution)/shard_map/ppermute | solution.py:24
  27.9 6.4 %collective-permute-start.9 = (f32[2,64,512]{2,1,0:T(8,128)S(1)}, f32[2,64,512]{2,1,0:T(8,128)S(1)}, u32[]{:S(2)}, u32[]{:S(2)}) collective-permute-start(f32[2,64,512]{2,1,0:T(8,128)S(1)} %collective-permute-done.6.refs_3_), channel_id=1, source_target_pairs={{0,2},{1,15},{2,4},{3,1},{4,6},{5,3},{6,8},{7,5},{8,10},{9,7},{10,... | collective-permute-start | bytes 786440 | tf_op jit(solution)/shard_map/ppermute | solution.py:24
  30.6 8.2 %collective-permute-start.13 = (f32[128,512]{1,0:T(8,128)S(1)}, f32[128,512]{1,0:T(8,128)S(1)}, u32[]{:S(2)}, u32[]{:S(2)}) collective-permute-start(f32[128,512]{1,0:T(8,128)S(1)} %get-tuple-element.43), channel_id=1, source_target_pairs={{0,32},{1,33},{2,34},{3,35},{4,36},{5,37},{6,38},{7,39},{8,40},{9,... | collective-permute-start | bytes 786440 | tf_op jit(solution)/shard_map/ppermute | solution.py:24
  32.7 6.1 %collective-permute-start.11 = (f32[2,64,512]{2,1,0:T(8,128)S(1)}, f32[2,64,512]{2,1,0:T(8,128)S(1)}, u32[]{:S(2)}, u32[]{:S(2)}) collective-permute-start(f32[2,64,512]{2,1,0:T(8,128)S(1)} %collective-permute-done.8.refs_4_), channel_id=1, source_target_pairs={{0,2},{1,15},{2,4},{3,1},{4,6},{5,3},{6,8},{7,5},{8,10},{9,7},{10,... | collective-permute-start | bytes 786440 | tf_op jit(solution)/shard_map/ppermute | solution.py:24
  34.3 6.7 %collective-permute-start.12 = (f32[2,64,512]{2,1,0:T(8,128)S(1)}, f32[2,64,512]{2,1,0:T(8,128)S(1)}, u32[]{:S(2)}, u32[]{:S(2)}) collective-permute-start(f32[2,64,512]{2,1,0:T(8,128)S(1)} %collective-permute-done.9.refs_5_), channel_id=1, source_target_pairs={{0,2},{1,15},{2,4},{3,1},{4,6},{5,3},{6,8},{7,5},{8,10},{9,7},{10,... | collective-permute-start | bytes 786440 | tf_op jit(solution)/shard_map/ppermute | solution.py:24
  37.4 7.2 %collective-permute-start.14 = (f32[128,512]{1,0:T(8,128)S(1)}, f32[128,512]{1,0:T(8,128)S(1)}, u32[]{:S(2)}, u32[]{:S(2)}) collective-permute-start(f32[128,512]{1,0:T(8,128)S(1)} %get-tuple-element.37.refs_0_), channel_id=1, source_target_pairs={{0,1},{1,0},{2,3},{3,2},{4,5},{5,4},{6,7},{7,6},{8,9},{9,8},{10,11... | collective-permute-start | bytes 786440 | tf_op jit(solution)/shard_map/ppermute | solution.py:24
  37.4 7.2 %collective-permute-start.16 = (f32[128,512]{1,0:T(8,128)S(1)}, f32[128,512]{1,0:T(8,128)S(1)}, u32[]{:S(2)}, u32[]{:S(2)}) collective-permute-start(f32[128,512]{1,0:T(8,128)S(1)} %collective-permute-done.7.refs_2_), channel_id=1, source_target_pairs={{0,1},{1,0},{2,3},{3,2},{4,5},{5,4},{6,7},{7,6},{8,9},{9,8},{10,11... | collective-permute-start | bytes 786440 | tf_op jit(solution)/shard_map/ppermute | solution.py:24
  38.8 5.8 %collective-permute-start.17 = (f32[128,512]{1,0:T(8,128)S(1)}, f32[128,512]{1,0:T(8,128)S(1)}, u32[]{:S(2)}, u32[]{:S(2)}) collective-permute-start(f32[128,512]{1,0:T(8,128)S(1)} %collective-permute-done.10.refs_3_), channel_id=1, source_target_pairs={{0,1},{1,0},{2,3},{3,2},{4,5},{5,4},{6,7},{7,6},{8,9},{9,8},{10,11... | collective-permute-start | bytes 786440 | tf_op jit(solution)/shard_map/ppermute | solution.py:24
  41.0 4.1 %collective-permute-start.15 = (f32[128,512]{1,0:T(8,128)S(1)}, f32[128,512]{1,0:T(8,128)S(1)}, u32[]{:S(2)}, u32[]{:S(2)}) collective-permute-start(f32[128,512]{1,0:T(8,128)S(1)} %collective-permute-done.13.refs_1_), channel_id=1, source_target_pairs={{0,1},{1,0},{2,3},{3,2},{4,5},{5,4},{6,7},{7,6},{8,9},{9,8},{10,11... | collective-permute-start | bytes 786440 | tf_op jit(solution)/shard_map/ppermute | solution.py:24
  44.0 5.8 %collective-permute-start.18 = (f32[2,64,512]{2,1,0:T(8,128)S(1)}, f32[2,64,512]{2,1,0:T(8,128)S(1)}, u32[]{:S(2)}, u32[]{:S(2)}) collective-permute-start(f32[2,64,512]{2,1,0:T(8,128)S(1)} %pad_maximum_fusion.2), channel_id=1, source_target_pairs={{0,2},{1,15},{2,4},{3,1},{4,6},{5,3},{6,8},{7,5},{8,10},{9,7},{10,... | collective-permute-start | bytes 786440 | tf_op jit(solution)/shard_map/ppermute | solution.py:24
  49.8 4.1 %collective-permute-start.19 = (f32[7,64,256]{2,1,0:T(8,128)S(1)}, f32[7,64,256]{2,1,0:T(8,128)S(1)}, u32[]{:S(2)}, u32[]{:S(2)}) collective-permute-start(f32[7,64,256]{2,1,0:T(8,128)S(1)} %get-tuple-element.51), channel_id=1, source_target_pairs={{0,1},{1,0},{2,3},{3,2},{4,5},{5,4},{6,7},{7,6},{8,9},{9,8},{10,11... | collective-permute-start | bytes 1376264 | tf_op jit(solution)/shard_map/ppermute | solution.py:24
  52.6 1.3 %collective-permute-start.20 = (f32[1,64,256]{2,1,0:T(8,128)S(1)}, f32[1,64,256]{2,1,0:T(8,128)S(1)}, u32[]{:S(2)}, u32[]{:S(2)}) collective-permute-start(f32[1,64,256]{2,1,0:T(8,128)S(1)} %get-tuple-element.52), channel_id=1, source_target_pairs={{0,1},{1,0},{2,3},{3,2},{4,5},{5,4},{6,7},{7,6},{8,9},{9,8},{10,11... | collective-permute-start | bytes 196616 | tf_op jit(solution)/shard_map/ppermute | solution.py:24
  54.5 7.7 %collective-permute-start.23 = (f32[2,64,256]{2,1,0:T(8,128)S(1)}, f32[2,64,256]{2,1,0:T(8,128)S(1)}, u32[]{:S(2)}, u32[]{:S(2)}) collective-permute-start(f32[2,64,256]{2,1,0:T(8,128)S(1)} %get-tuple-element.56), channel_id=1, source_target_pairs={{0,192},{1,193},{2,194},{3,195},{4,196},{5,197},{6,198},{7,199},{8... | collective-permute-start | bytes 393224 | tf_op jit(solution)/shard_map/ppermute | solution.py:24
  57.1 6.2 %collective-permute-start.22 = (f32[2,64,256]{2,1,0:T(8,128)S(1)}, f32[2,64,256]{2,1,0:T(8,128)S(1)}, u32[]{:S(2)}, u32[]{:S(2)}) collective-permute-start(f32[2,64,256]{2,1,0:T(8,128)S(1)} %get-tuple-element.55), channel_id=1, source_target_pairs={{0,128},{1,129},{2,130},{3,131},{4,132},{5,133},{6,134},{7,135},{8... | collective-permute-start | bytes 393224 | tf_op jit(solution)/shard_map/ppermute | solution.py:24
  57.6 10.0 %collective-permute-start.21 = (f32[2,64,256]{2,1,0:T(8,128)S(1)}, f32[2,64,256]{2,1,0:T(8,128)S(1)}, u32[]{:S(2)}, u32[]{:S(2)}) collective-permute-start(f32[2,64,256]{2,1,0:T(8,128)S(1)} %get-tuple-element.54), channel_id=1, source_target_pairs={{0,64},{1,65},{2,66},{3,67},{4,68},{5,69},{6,70},{7,71},{8,72},{9,... | collective-permute-start | bytes 393224 | tf_op jit(solution)/shard_map/ppermute | solution.py:24
  58.2 12.4 %collective-permute-start.27 = (f32[2,64,256]{2,1,0:T(8,128)S(1)}, f32[2,64,256]{2,1,0:T(8,128)S(1)}, u32[]{:S(2)}, u32[]{:S(2)}) collective-permute-start(f32[2,64,256]{2,1,0:T(8,128)S(1)} %get-tuple-element.60), channel_id=1, source_target_pairs={{0,192},{1,193},{2,194},{3,195},{4,196},{5,197},{6,198},{7,199},{8... | collective-permute-start | bytes 393224 | tf_op jit(solution)/shard_map/ppermute | solution.py:24
  60.3 10.4 %collective-permute-start.26 = (f32[2,64,256]{2,1,0:T(8,128)S(1)}, f32[2,64,256]{2,1,0:T(8,128)S(1)}, u32[]{:S(2)}, u32[]{:S(2)}) collective-permute-start(f32[2,64,256]{2,1,0:T(8,128)S(1)} %get-tuple-element.59), channel_id=1, source_target_pairs={{0,128},{1,129},{2,130},{3,131},{4,132},{5,133},{6,134},{7,135},{8... | collective-permute-start | bytes 393224 | tf_op jit(solution)/shard_map/ppermute | solution.py:24
  62.3 10.1 %collective-permute-start.25 = (f32[2,64,256]{2,1,0:T(8,128)S(1)}, f32[2,64,256]{2,1,0:T(8,128)S(1)}, u32[]{:S(2)}, u32[]{:S(2)}) collective-permute-start(f32[2,64,256]{2,1,0:T(8,128)S(1)} %get-tuple-element.58), channel_id=1, source_target_pairs={{0,64},{1,65},{2,66},{3,67},{4,68},{5,69},{6,70},{7,71},{8,72},{9,... | collective-permute-start | bytes 393224 | tf_op jit(solution)/shard_map/ppermute | solution.py:24
  67.6 7.6 %collective-permute-start.24 = (f32[2,64,256]{2,1,0:T(8,128)S(1)}, f32[2,64,256]{2,1,0:T(8,128)S(1)}, u32[]{:S(2)}, u32[]{:S(2)}) collective-permute-start(f32[2,64,256]{2,1,0:T(8,128)S(1)} %add_add_fusion.1), channel_id=1, source_target_pairs={{0,32},{1,48},{2,34},{3,50},{4,36},{5,52},{6,38},{7,54},{8,40},{9,... | collective-permute-start | bytes 393224 | tf_op jit(solution)/shard_map/ppermute | solution.py:24
  72.3 7.7 %copy-start.3 = (s32[2,16]{1,0:T(2,128)S(1)}, s32[2,16]{1,0:T(2,128)}, u32[]{:S(2)}) copy-start(s32[2,16]{1,0:T(2,128)} %pattern_ref.7) | copy-start | bytes 388
  72.3 6.3 %collective-permute-start.28 = (f32[2,64,256]{2,1,0:T(8,128)S(1)}, f32[2,64,256]{2,1,0:T(8,128)S(1)}, u32[]{:S(2)}, u32[]{:S(2)}) collective-permute-start(f32[2,64,256]{2,1,0:T(8,128)S(1)} %add_add_fusion), channel_id=1, source_target_pairs={{0,0},{1,16},{2,2},{3,18},{4,4},{5,20},{6,6},{7,22},{8,8},{9,24},{... | collective-permute-start | bytes 393224 | tf_op jit(solution)/shard_map/ppermute | solution.py:24
  75.2 3.4 %collective-permute-start.29 = (f32[2,64,256]{2,1,0:T(8,128)S(1)}, f32[2,64,256]{2,1,0:T(8,128)S(1)}, u32[]{:S(2)}, u32[]{:S(2)}) collective-permute-start(f32[2,64,256]{2,1,0:T(8,128)S(1)} %collective-permute-done.24.own_flip), channel_id=1, source_target_pairs={{0,1},{1,0},{2,3},{3,2},{4,5},{5,4},{6,7},{7,6},{8,9},{9,8},{10,11... | collective-permute-start | bytes 393224 | tf_op jit(solution)/shard_map/ppermute | solution.py:24
  78.6 1.3 %collective-permute-start.30 = (f32[2,64,256]{2,1,0:T(8,128)S(1)}, f32[2,64,256]{2,1,0:T(8,128)S(1)}, u32[]{:S(2)}, u32[]{:S(2)}) collective-permute-start(f32[2,64,256]{2,1,0:T(8,128)S(1)} %collective-permute-done.28.own_same), channel_id=1, source_target_pairs={{0,1},{1,0},{2,3},{3,2},{4,5},{5,4},{6,7},{7,6},{8,9},{9,8},{10,11... | collective-permute-start | bytes 393224 | tf_op jit(solution)/shard_map/ppermute | solution.py:24

commit v4 on v3

--- a/solution.py
+++ b/solution.py
@@ -10,7 +10,7 @@
 F32 = jnp.float32
 BF16 = jnp.bfloat16
 AXES = ("prow", "pcol")
-VMEM_LIMIT = 40 * 1024 * 1024
+VMEM_LIMIT = 24 * 1024 * 1024
 
 DEVICES = [(x, y, z, c) for x in range(4) for y in range(4) for z in range(8) for c in range(2)]
 
@@ -247,7 +247,7 @@
     a_high, a_low = call(split_inverse, [whole, whole], *blocks, *halves)
     keep_early, give_early = product(early, a_high, a_low)
     keep_late, give_late = product(late, a_high, a_low)
-    got_early = send(after(give_early, last), other_core)
+    got_early = send(give_early, other_core)
     got_late = send(give_late, other_core)
     terms = call(arrange, [((2, 64, B), F32)] * 8, keep_early, keep_late, got_early, got_late)
     moved = list(terms[:2]) + [send(terms[2 * m + i], along_x(m)) for i in range(2) for m in range(1, 4)]

time: 81.7 us -> 82.8 us (1.013)
  starting transfers between devices: 47.2 us -> 49.4 us
  waiting for transfers between devices: 25.2 us -> 23.1 us
  local copies, waits for them, and re-layouts: 1.97 us -> 2.85 us
    ppermute x31, starting transfers between devices: 47.2 us -> 49.4 us  [send(): return lax.ppermute(array, AXES, pairs)]
    ppermute x31, waiting for transfers between devices: 25.2 us -> 23.1 us  [send(): return lax.ppermute(array, AXES, pairs)]
    slice x2 -> x3, local copies, waits for them, and re-layouts: 0.02 us -> 0.89 us  [per_device(): last = send(jnp.concatenate([part[:1] for part in pairs]), ring)]
    unnamed x8 -> x12, local copies, waits for them, and re-layouts: 1.91 us -> 1.92 us
  transfers between devices with their start and end apart: 31 -> 31, of which waited for: 16 -> 15; matrix products, arithmetic and copies ran while one was open for 0% -> 0% of each run, Pallas kernels for 5% -> 5%
where the time goes in v4:
time: 82.8 us; the launch traced here: 82.5 us
  starting transfers between devices  49.4 us (60%)
  waiting for transfers between devices  23.1 us (28%)
  Pallas kernels  6.81 us (8%)
  local copies, waits for them, and re-layouts  2.85 us (3%)
    ppermute x31, starting transfers between devices, send(): return lax.ppermute(array, AXES, pairs)  49.4 us
    ppermute x31, waiting for transfers between devices, send(): return lax.ppermute(array, AXES, pairs)  23.1 us
    pallas_call x8, Pallas kernels, call(): pl.pallas_call(kernel, out_shape=shapes, in_specs=in_specs, out_specs=[pl...  6.81 us
    unnamed x12, local copies, waits for them, and re-layouts  1.92 us
  transfers between devices with their start and end apart: 31, of which 15 were waited for; matrix products, arithmetic and copies ran while one was open for 0% of the time, Pallas kernels for 5%

profile of v4, /device:TPU:1, one launch (start us, length us, event | category | flops | bytes accessed | tf_op | source)
XLA Modules:
  0.0 82.5 jit_solution(8650462128508047872)
XLA Ops:
  0.0 1.2 %copy-done = f32[256,1024]{1,0:T(8,128)S(1)} copy-done((f32[256,1024]{1,0:T(8,128)S(1)}, f32[256,1024]{1,0:T(8,128)}, u32[]{:S(2)}) %copy-start) | copy-done | bytes 1048600
  1.2 0.7 copy-done.4
  1.9 0.6 shard_map.38
  2.6 3.3 %collective-permute-start.2 = (f32[2,128,512]{2,1,0:T(8,128)S(1)}, f32[2,128,512]{2,1,0:T(8,128)S(1)}, u32[]{:S(2)}, u32[]{:S(2)}) collective-permute-start(f32[2,128,512]{2,1,0:T(8,128)S(1)} %get-tuple-element.35), channel_id=1, source_target_pairs={{0,1},{1,0},{2,3},{3,2},{4,5},{5,4},{6,7},{7,6},{8,9},{9,8},{10,11... | collective-permute-start | bytes 1572872 | tf_op jit(solution)/shard_map/ppermute | solution.py:24
  5.9 0.6 shard_map.37
  6.5 1.9 %collective-permute-start = (f32[64,512]{1,0:T(8,128)S(1)}, f32[64,512]{1,0:T(8,128)S(1)}, u32[]{:S(2)}, u32[]{:S(2)}) collective-permute-start(f32[64,512]{1,0:T(8,128)S(1)} %get-tuple-element.32), channel_id=1, source_target_pairs={{0,0},{1,16},{2,2},{3,18},{4,4},{5,20},{6,6},{7,22},{8,8},{9,24},{... | collective-permute-start | bytes 393224 | tf_op jit(solution)/shard_map/ppermute | solution.py:24
  8.4 1.8 %collective-permute-start.1 = (f32[64,512]{1,0:T(8,128)S(1)}, f32[64,512]{1,0:T(8,128)S(1)}, u32[]{:S(2)}, u32[]{:S(2)}) collective-permute-start(f32[64,512]{1,0:T(8,128)S(1)} %get-tuple-element.33), channel_id=1, source_target_pairs={{0,32},{1,48},{2,34},{3,50},{4,36},{5,52},{6,38},{7,54},{8,40},{9,... | collective-permute-start | bytes 393224 | tf_op jit(solution)/shard_map/ppermute | solution.py:24
  10.2 0.6 shard_map.39
  10.9 2.2 %collective-permute-done = f32[64,512]{1,0:T(8,128)S(1)} collective-permute-done((f32[64,512]{1,0:T(8,128)S(1)}, f32[64,512]{1,0:T(8,128)S(1)}, u32[]{:S(2)}, u32[]{:S(2)}) %collective-permute-start) | collective-permute-done | bytes 131104 | tf_op jit(solution)/shard_map/ppermute | solution.py:24
  13.1 2.1 %collective-permute-done.1 = f32[64,512]{1,0:T(8,128)S(1)} collective-permute-done((f32[64,512]{1,0:T(8,128)S(1)}, f32[64,512]{1,0:T(8,128)S(1)}, u32[]{:S(2)}, u32[]{:S(2)}) %collective-permute-start.1) | collective-permute-done | bytes 131104 | tf_op jit(solution)/shard_map/ppermute | solution.py:24
  15.3 0.3 collective-permute-start.4
  15.6 0.8 %collective-permute-done.3 = f32[64,512]{1,0:T(8,128)S(1)} collective-permute-done((f32[64,512]{1,0:T(8,128)S(1)}, f32[64,512]{1,0:T(8,128)S(1)}, u32[]{:S(2)}, u32[]{:S(2)}) %collective-permute-start.3) | collective-permute-done | bytes 131104 | tf_op jit(solution)/shard_map/ppermute | solution.py:24
  16.7 4.4 %collective-permute-start.5 = (f32[2,64,512]{2,1,0:T(8,128)S(1)}, f32[2,64,512]{2,1,0:T(8,128)S(1)}, u32[]{:S(2)}, u32[]{:S(2)}) collective-permute-start(f32[2,64,512]{2,1,0:T(8,128)S(1)} %pad_maximum_fusion), channel_id=1, source_target_pairs={{0,2},{1,15},{2,4},{3,1},{4,6},{5,3},{6,8},{7,5},{8,10},{9,7},{10,... | collective-permute-start | bytes 786440 | tf_op jit(solution)/shard_map/ppermute | solution.py:24
  21.0 0.7 collective-permute-start.6
  21.8 2.5 %collective-permute-start.10 = (f32[128,512]{1,0:T(8,128)S(1)}, f32[128,512]{1,0:T(8,128)S(1)}, u32[]{:S(2)}, u32[]{:S(2)}) collective-permute-start(f32[128,512]{1,0:T(8,128)S(1)} %get-tuple-element.42), channel_id=1, source_target_pairs={{0,48},{1,49},{2,50},{3,51},{4,52},{5,53},{6,54},{7,55},{8,56},{9,... | collective-permute-start | bytes 786440 | tf_op jit(solution)/shard_map/ppermute | solution.py:24
  24.4 3.5 %collective-permute-start.8 = (f32[2,64,512]{2,1,0:T(8,128)S(1)}, f32[2,64,512]{2,1,0:T(8,128)S(1)}, u32[]{:S(2)}, u32[]{:S(2)}) collective-permute-start(f32[2,64,512]{2,1,0:T(8,128)S(1)} %collective-permute-done.5.refs_2_), channel_id=1, source_target_pairs={{0,2},{1,15},{2,4},{3,1},{4,6},{5,3},{6,8},{7,5},{8,10},{9,7},{10,... | collective-permute-start | bytes 786440 | tf_op jit(solution)/shard_map/ppermute | solution.py:24
  27.9 2.7 %collective-permute-start.9 = (f32[2,64,512]{2,1,0:T(8,128)S(1)}, f32[2,64,512]{2,1,0:T(8,128)S(1)}, u32[]{:S(2)}, u32[]{:S(2)}) collective-permute-start(f32[2,64,512]{2,1,0:T(8,128)S(1)} %collective-permute-done.6.refs_3_), channel_id=1, source_target_pairs={{0,2},{1,15},{2,4},{3,1},{4,6},{5,3},{6,8},{7,5},{8,10},{9,7},{10,... | collective-permute-start | bytes 786440 | tf_op jit(solution)/shard_map/ppermute | solution.py:24
  30.6 2.1 %collective-permute-start.13 = (f32[128,512]{1,0:T(8,128)S(1)}, f32[128,512]{1,0:T(8,128)S(1)}, u32[]{:S(2)}, u32[]{:S(2)}) collective-permute-start(f32[128,512]{1,0:T(8,128)S(1)} %get-tuple-element.42), channel_id=1, source_target_pairs={{0,32},{1,33},{2,34},{3,35},{4,36},{5,37},{6,38},{7,39},{8,40},{9,... | collective-permute-start | bytes 786440 | tf_op jit(solution)/shard_map/ppermute | solution.py:24
  32.7 1.6 %collective-permute-start.11 = (f32[2,64,512]{2,1,0:T(8,128)S(1)}, f32[2,64,512]{2,1,0:T(8,128)S(1)}, u32[]{:S(2)}, u32[]{:S(2)}) collective-permute-start(f32[2,64,512]{2,1,0:T(8,128)S(1)} %collective-permute-done.8.refs_4_), channel_id=1, source_target_pairs={{0,2},{1,15},{2,4},{3,1},{4,6},{5,3},{6,8},{7,5},{8,10},{9,7},{10,... | collective-permute-start | bytes 786440 | tf_op jit(solution)/shard_map/ppermute | solution.py:24
  34.3 3.1 %collective-permute-start.12 = (f32[2,64,512]{2,1,0:T(8,128)S(1)}, f32[2,64,512]{2,1,0:T(8,128)S(1)}, u32[]{:S(2)}, u32[]{:S(2)}) collective-permute-start(f32[2,64,512]{2,1,0:T(8,128)S(1)} %collective-permute-done.9.refs_5_), channel_id=1, source_target_pairs={{0,2},{1,15},{2,4},{3,1},{4,6},{5,3},{6,8},{7,5},{8,10},{9,7},{10,... | collective-permute-start | bytes 786440 | tf_op jit(solution)/shard_map/ppermute | solution.py:24
  37.4 0.5 collective-permute-start.16
  37.9 0.9 %collective-permute-done.13.refs_1_ = f32[128,512]{1,0:T(8,128)S(1)} collective-permute-done((f32[128,512]{1,0:T(8,128)S(1)}, f32[128,512]{1,0:T(8,128)S(1)}, u32[]{:S(2)}, u32[]{:S(2)}) %collective-permute-start.13) | collective-permute-done | bytes 262176 | tf_op jit(solution)/shard_map/ppermute | solution.py:24
  38.8 2.2 %collective-permute-done.12.refs_7_ = f32[2,64,512]{2,1,0:T(8,128)S(1)} collective-permute-done((f32[2,64,512]{2,1,0:T(8,128)S(1)}, f32[2,64,512]{2,1,0:T(8,128)S(1)}, u32[]{:S(2)}, u32[]{:S(2)}) %collective-permute-start.12) | collective-permute-done | bytes 262176 | tf_op jit(solution)/shard_map/ppermute | solution.py:24
  41.0 2.9 %collective-permute-start.15 = (f32[128,512]{1,0:T(8,128)S(1)}, f32[128,512]{1,0:T(8,128)S(1)}, u32[]{:S(2)}, u32[]{:S(2)}) collective-permute-start(f32[128,512]{1,0:T(8,128)S(1)} %collective-permute-done.13.refs_1_), channel_id=1, source_target_pairs={{0,1},{1,0},{2,3},{3,2},{4,5},{5,4},{6,7},{7,6},{8,9},{9,8},{10,11... | collective-permute-start | bytes 786440 | tf_op jit(solution)/shard_map/ppermute | solution.py:24
  44.1 0.9 %slice-done = f32[1,64,512]{2,1,0:T(8,128)S(1)} async-done(((f32[2,64,512]{2,1,0:T(8,128)}), f32[1,64,512]{2,1,0:T(8,128)S(1)}, s32[]{:S(2)}) %slice-start) | async-done | bytes 131096 | tf_op jit(solution)/shard_map/slice | solution.py:241
  45.0 0.8 collective-permute-start.18
  45.8 0.6 shard_map.40
  46.4 1.6 %shard_map.41 = (f32[7,64,256]{2,1,0:T(8,128)S(1)}, f32[7,64,256]{2,1,0:T(8,128)S(1)}) custom-call(f32[1,64,512]{2,1,0:T(8,128)S(1)} %slice.18.refs_0_, f32[1,64,512]{2,1,0:T(8,128)S(1)} %slice.19.refs_1_, f32[2,64,512]{2,1,0:T(8,128)S(1)} %collective-permute-done.5.refs_2_, f32[2,64,512]{2,1,0:T(8,128)S(1)} %collective-permute-done.6.refs_3_, ...), custom_call_target="tpu_custom_call" | custom-call | flops 1409286144 | bytes 4849664 | tf_op jit(solution)/shard_map/pallas_call | solution.py:66
  48.2 2.5 %collective-permute-done.18 = f32[2,64,512]{2,1,0:T(8,128)S(1)} collective-permute-done((f32[2,64,512]{2,1,0:T(8,128)S(1)}, f32[2,64,512]{2,1,0:T(8,128)S(1)}, u32[]{:S(2)}, u32[]{:S(2)}) %collective-permute-start.18) | collective-permute-done | bytes 262176 | tf_op jit(solution)/shard_map/ppermute | solution.py:24
  50.8 0.6 shard_map.42
  51.4 2.8 %collective-permute-start.20 = (f32[1,64,256]{2,1,0:T(8,128)S(1)}, f32[1,64,256]{2,1,0:T(8,128)S(1)}, u32[]{:S(2)}, u32[]{:S(2)}) collective-permute-start(f32[1,64,256]{2,1,0:T(8,128)S(1)} %get-tuple-element.50), channel_id=1, source_target_pairs={{0,1},{1,0},{2,3},{3,2},{4,5},{5,4},{6,7},{7,6},{8,9},{9,8},{10,11... | collective-permute-start | bytes 196616 | tf_op jit(solution)/shard_map/ppermute | solution.py:24
  54.2 0.9 %collective-permute-done.20.got_late = f32[1,64,256]{2,1,0:T(8,128)S(1)} collective-permute-done((f32[1,64,256]{2,1,0:T(8,128)S(1)}, f32[1,64,256]{2,1,0:T(8,128)S(1)}, u32[]{:S(2)}, u32[]{:S(2)}) %collective-permute-start.20) | collective-permute-done | bytes 65568 | tf_op jit(solution)/shard_map/ppermute | solution.py:24
  55.1 0.6 shard_map.43
  55.7 2.5 %collective-permute-start.23 = (f32[2,64,256]{2,1,0:T(8,128)S(1)}, f32[2,64,256]{2,1,0:T(8,128)S(1)}, u32[]{:S(2)}, u32[]{:S(2)}) collective-permute-start(f32[2,64,256]{2,1,0:T(8,128)S(1)} %get-tuple-element.54), channel_id=1, source_target_pairs={{0,192},{1,193},{2,194},{3,195},{4,196},{5,197},{6,198},{7,199},{8... | collective-permute-start | bytes 393224 | tf_op jit(solution)/shard_map/ppermute | solution.py:24
  58.3 0.5 collective-permute-start.22
  58.8 0.6 collective-permute-start.21
  59.4 2.1 %collective-permute-start.27 = (f32[2,64,256]{2,1,0:T(8,128)S(1)}, f32[2,64,256]{2,1,0:T(8,128)S(1)}, u32[]{:S(2)}, u32[]{:S(2)}) collective-permute-start(f32[2,64,256]{2,1,0:T(8,128)S(1)} %get-tuple-element.58), channel_id=1, source_target_pairs={{0,192},{1,193},{2,194},{3,195},{4,196},{5,197},{6,198},{7,199},{8... | collective-permute-start | bytes 393224 | tf_op jit(solution)/shard_map/ppermute | solution.py:24
  61.4 1.2 %collective-permute-start.26 = (f32[2,64,256]{2,1,0:T(8,128)S(1)}, f32[2,64,256]{2,1,0:T(8,128)S(1)}, u32[]{:S(2)}, u32[]{:S(2)}) collective-permute-start(f32[2,64,256]{2,1,0:T(8,128)S(1)} %get-tuple-element.57), channel_id=1, source_target_pairs={{0,128},{1,129},{2,130},{3,131},{4,132},{5,133},{6,134},{7,135},{8... | collective-permute-start | bytes 393224 | tf_op jit(solution)/shard_map/ppermute | solution.py:24
  62.7 1.4 %collective-permute-done.22 = f32[2,64,256]{2,1,0:T(8,128)S(1)} collective-permute-done((f32[2,64,256]{2,1,0:T(8,128)S(1)}, f32[2,64,256]{2,1,0:T(8,128)S(1)}, u32[]{:S(2)}, u32[]{:S(2)}) %collective-permute-start.22) | collective-permute-done | bytes 131104 | tf_op jit(solution)/shard_map/ppermute | solution.py:24
  64.1 4.9 %collective-permute-done.21 = f32[2,64,256]{2,1,0:T(8,128)S(1)} collective-permute-done((f32[2,64,256]{2,1,0:T(8,128)S(1)}, f32[2,64,256]{2,1,0:T(8,128)S(1)}, u32[]{:S(2)}, u32[]{:S(2)}) %collective-permute-start.21) | collective-permute-done | bytes 131104 | tf_op jit(solution)/shard_map/ppermute | solution.py:24
  69.1 3.6 %collective-permute-start.24 = (f32[2,64,256]{2,1,0:T(8,128)S(1)}, f32[2,64,256]{2,1,0:T(8,128)S(1)}, u32[]{:S(2)}, u32[]{:S(2)}) collective-permute-start(f32[2,64,256]{2,1,0:T(8,128)S(1)} %add_add_fusion.1), channel_id=1, source_target_pairs={{0,32},{1,48},{2,34},{3,50},{4,36},{5,52},{6,38},{7,54},{8,40},{9,... | collective-permute-start | bytes 393224 | tf_op jit(solution)/shard_map/ppermute | solution.py:24
  72.7 0.6 collective-permute-done.25
  73.3 3.0 %collective-permute-start.28 = (f32[2,64,256]{2,1,0:T(8,128)S(1)}, f32[2,64,256]{2,1,0:T(8,128)S(1)}, u32[]{:S(2)}, u32[]{:S(2)}) collective-permute-start(f32[2,64,256]{2,1,0:T(8,128)S(1)} %add_add_fusion), channel_id=1, source_target_pairs={{0,0},{1,16},{2,2},{3,18},{4,4},{5,20},{6,6},{7,22},{8,8},{9,24},{... | collective-permute-start | bytes 393224 | tf_op jit(solution)/shard_map/ppermute | solution.py:24
  76.4 0.4 collective-permute-done.24.own_flip
  76.7 0.3 collective-permute-start.29
  77.0 2.6 %collective-permute-done.28.own_same = f32[2,64,256]{2,1,0:T(8,128)S(1)} collective-permute-done((f32[2,64,256]{2,1,0:T(8,128)S(1)}, f32[2,64,256]{2,1,0:T(8,128)S(1)}, u32[]{:S(2)}, u32[]{:S(2)}) %collective-permute-start.28) | collective-permute-done | bytes 131104 | tf_op jit(solution)/shard_map/ppermute | solution.py:24
  79.6 1.3 %collective-permute-done.30.got_same = f32[2,64,256]{2,1,0:T(8,128)S(1)} collective-permute-done((f32[2,64,256]{2,1,0:T(8,128)S(1)}, f32[2,64,256]{2,1,0:T(8,128)S(1)}, u32[]{:S(2)}, u32[]{:S(2)}) %collective-permute-start.30) | collective-permute-done | bytes 131104 | tf_op jit(solution)/shard_map/ppermute | solution.py:24
  81.0 1.5 %shard_map.44 = f32[256,2,256]{2,1,0:T(2,128)} custom-call(s32[2,16]{1,0:T(2,128)S(1)} %copy-done.5, f32[2,64,256]{2,1,0:T(8,128)S(1)} %collective-permute-done.24.own_flip, f32[2,64,256]{2,1,0:T(8,128)S(1)} %collective-permute-done.28.own_same, f32[2,64,256]{2,1,0:T(8,128)S(1)} %collective-permute-done.29.got_flip, ...), custom_call_target="tpu_custom_call" | custom-call | bytes 1048704 | tf_op jit(solution)/shard_map/pallas_call | solution.py:66
  (45 shorter events, 1.0 us)
Async XLA Ops:
  0.0 1.2 %copy-start = (f32[256,1024]{1,0:T(8,128)S(1)}, f32[256,1024]{1,0:T(8,128)}, u32[]{:S(2)}) copy-start(f32[256,1024]{1,0:T(8,128)} %inverse_ref.1) | copy-start | bytes 3145732
  1.2 0.7 copy-start.4
  1.9 4.0 %copy-start.1 = (f32[1024,2,64]{0,2,1:T(8,128)S(1)}, f32[1024,2,64]{0,2,1:T(8,128)}, u32[]{:S(2)}) copy-start(f32[1024,2,64]{0,2,1:T(8,128)} %param.4) | copy-start | bytes 1572868
  2.6 7.7 %collective-permute-start.2 = (f32[2,128,512]{2,1,0:T(8,128)S(1)}, f32[2,128,512]{2,1,0:T(8,128)S(1)}, u32[]{:S(2)}, u32[]{:S(2)}) collective-permute-start(f32[2,128,512]{2,1,0:T(8,128)S(1)} %get-tuple-element.35), channel_id=1, source_target_pairs={{0,1},{1,0},{2,3},{3,2},{4,5},{5,4},{6,7},{7,6},{8,9},{9,8},{10,11... | collective-permute-start | bytes 1572872 | tf_op jit(solution)/shard_map/ppermute | solution.py:24
  6.5 6.6 %collective-permute-start = (f32[64,512]{1,0:T(8,128)S(1)}, f32[64,512]{1,0:T(8,128)S(1)}, u32[]{:S(2)}, u32[]{:S(2)}) collective-permute-start(f32[64,512]{1,0:T(8,128)S(1)} %get-tuple-element.32), channel_id=1, source_target_pairs={{0,0},{1,16},{2,2},{3,18},{4,4},{5,20},{6,6},{7,22},{8,8},{9,24},{... | collective-permute-start | bytes 393224 | tf_op jit(solution)/shard_map/ppermute | solution.py:24
  8.4 6.7 %collective-permute-start.1 = (f32[64,512]{1,0:T(8,128)S(1)}, f32[64,512]{1,0:T(8,128)S(1)}, u32[]{:S(2)}, u32[]{:S(2)}) collective-permute-start(f32[64,512]{1,0:T(8,128)S(1)} %get-tuple-element.33), channel_id=1, source_target_pairs={{0,32},{1,48},{2,34},{3,50},{4,36},{5,52},{6,38},{7,54},{8,40},{9,... | collective-permute-start | bytes 393224 | tf_op jit(solution)/shard_map/ppermute | solution.py:24
  15.1 1.3 %collective-permute-start.3 = (f32[64,512]{1,0:T(8,128)S(1)}, f32[64,512]{1,0:T(8,128)S(1)}, u32[]{:S(2)}, u32[]{:S(2)}) collective-permute-start(f32[64,512]{1,0:T(8,128)S(1)} %collective-permute-done), channel_id=1, source_target_pairs={{0,1},{1,0},{2,3},{3,2},{4,5},{5,4},{6,7},{7,6},{8,9},{9,8},{10,11... | collective-permute-start | bytes 393224 | tf_op jit(solution)/shard_map/ppermute | solution.py:24
  15.3 1.4 %collective-permute-start.4 = (f32[64,512]{1,0:T(8,128)S(1)}, f32[64,512]{1,0:T(8,128)S(1)}, u32[]{:S(2)}, u32[]{:S(2)}) collective-permute-start(f32[64,512]{1,0:T(8,128)S(1)} %collective-permute-done.1), channel_id=1, source_target_pairs={{0,1},{1,0},{2,3},{3,2},{4,5},{5,4},{6,7},{7,6},{8,9},{9,8},{10,11... | collective-permute-start | bytes 393224 | tf_op jit(solution)/shard_map/ppermute | solution.py:24
  15.6 8.6 %collective-permute-start.7 = (f32[128,512]{1,0:T(8,128)S(1)}, f32[128,512]{1,0:T(8,128)S(1)}, u32[]{:S(2)}, u32[]{:S(2)}) collective-permute-start(f32[128,512]{1,0:T(8,128)S(1)} %get-tuple-element.36.refs_0_), channel_id=1, source_target_pairs={{0,16},{1,17},{2,18},{3,19},{4,20},{5,21},{6,22},{7,23},{8,24},{9,... | collective-permute-start | bytes 786440 | tf_op jit(solution)/shard_map/ppermute | solution.py:24
  16.7 7.7 %collective-permute-start.5 = (f32[2,64,512]{2,1,0:T(8,128)S(1)}, f32[2,64,512]{2,1,0:T(8,128)S(1)}, u32[]{:S(2)}, u32[]{:S(2)}) collective-permute-start(f32[2,64,512]{2,1,0:T(8,128)S(1)} %pad_maximum_fusion), channel_id=1, source_target_pairs={{0,2},{1,15},{2,4},{3,1},{4,6},{5,3},{6,8},{7,5},{8,10},{9,7},{10,... | collective-permute-start | bytes 786440 | tf_op jit(solution)/shard_map/ppermute | solution.py:24
  21.0 6.8 %collective-permute-start.6 = (f32[2,64,512]{2,1,0:T(8,128)S(1)}, f32[2,64,512]{2,1,0:T(8,128)S(1)}, u32[]{:S(2)}, u32[]{:S(2)}) collective-permute-start(f32[2,64,512]{2,1,0:T(8,128)S(1)} %pad_maximum_fusion.1), channel_id=1, source_target_pairs={{0,2},{1,15},{2,4},{3,1},{4,6},{5,3},{6,8},{7,5},{8,10},{9,7},{10,... | collective-permute-start | bytes 786440 | tf_op jit(solution)/shard_map/ppermute | solution.py:24
  21.8 10.9 %collective-permute-start.10 = (f32[128,512]{1,0:T(8,128)S(1)}, f32[128,512]{1,0:T(8,128)S(1)}, u32[]{:S(2)}, u32[]{:S(2)}) collective-permute-start(f32[128,512]{1,0:T(8,128)S(1)} %get-tuple-element.42), channel_id=1, source_target_pairs={{0,48},{1,49},{2,50},{3,51},{4,52},{5,53},{6,54},{7,55},{8,56},{9,... | collective-permute-start | bytes 786440 | tf_op jit(solution)/shard_map/ppermute | solution.py:24
  24.4 8.4 %collective-permute-start.8 = (f32[2,64,512]{2,1,0:T(8,128)S(1)}, f32[2,64,512]{2,1,0:T(8,128)S(1)}, u32[]{:S(2)}, u32[]{:S(2)}) collective-permute-start(f32[2,64,512]{2,1,0:T(8,128)S(1)} %collective-permute-done.5.refs_2_), channel_id=1, source_target_pairs={{0,2},{1,15},{2,4},{3,1},{4,6},{5,3},{6,8},{7,5},{8,10},{9,7},{10,... | collective-permute-start | bytes 786440 | tf_op jit(solution)/shard_map/ppermute | solution.py:24
  27.9 6.4 %collective-permute-start.9 = (f32[2,64,512]{2,1,0:T(8,128)S(1)}, f32[2,64,512]{2,1,0:T(8,128)S(1)}, u32[]{:S(2)}, u32[]{:S(2)}) collective-permute-start(f32[2,64,512]{2,1,0:T(8,128)S(1)} %collective-permute-done.6.refs_3_), channel_id=1, source_target_pairs={{0,2},{1,15},{2,4},{3,1},{4,6},{5,3},{6,8},{7,5},{8,10},{9,7},{10,... | collective-permute-start | bytes 786440 | tf_op jit(solution)/shard_map/ppermute | solution.py:24
  30.6 8.2 %collective-permute-start.13 = (f32[128,512]{1,0:T(8,128)S(1)}, f32[128,512]{1,0:T(8,128)S(1)}, u32[]{:S(2)}, u32[]{:S(2)}) collective-permute-start(f32[128,512]{1,0:T(8,128)S(1)} %get-tuple-element.42), channel_id=1, source_target_pairs={{0,32},{1,33},{2,34},{3,35},{4,36},{5,37},{6,38},{7,39},{8,40},{9,... | collective-permute-start | bytes 786440 | tf_op jit(solution)/shard_map/ppermute | solution.py:24
  32.7 6.1 %collective-permute-start.11 = (f32[2,64,512]{2,1,0:T(8,128)S(1)}, f32[2,64,512]{2,1,0:T(8,128)S(1)}, u32[]{:S(2)}, u32[]{:S(2)}) collective-permute-start(f32[2,64,512]{2,1,0:T(8,128)S(1)} %collective-permute-done.8.refs_4_), channel_id=1, source_target_pairs={{0,2},{1,15},{2,4},{3,1},{4,6},{5,3},{6,8},{7,5},{8,10},{9,7},{10,... | collective-permute-start | bytes 786440 | tf_op jit(solution)/shard_map/ppermute | solution.py:24
  34.3 6.7 %collective-permute-start.12 = (f32[2,64,512]{2,1,0:T(8,128)S(1)}, f32[2,64,512]{2,1,0:T(8,128)S(1)}, u32[]{:S(2)}, u32[]{:S(2)}) collective-permute-start(f32[2,64,512]{2,1,0:T(8,128)S(1)} %collective-permute-done.9.refs_5_), channel_id=1, source_target_pairs={{0,2},{1,15},{2,4},{3,1},{4,6},{5,3},{6,8},{7,5},{8,10},{9,7},{10,... | collective-permute-start | bytes 786440 | tf_op jit(solution)/shard_map/ppermute | solution.py:24
  37.4 8.3 %collective-permute-start.14 = (f32[128,512]{1,0:T(8,128)S(1)}, f32[128,512]{1,0:T(8,128)S(1)}, u32[]{:S(2)}, u32[]{:S(2)}) collective-permute-start(f32[128,512]{1,0:T(8,128)S(1)} %get-tuple-element.36.refs_0_), channel_id=1, source_target_pairs={{0,1},{1,0},{2,3},{3,2},{4,5},{5,4},{6,7},{7,6},{8,9},{9,8},{10,11... | collective-permute-start | bytes 786440 | tf_op jit(solution)/shard_map/ppermute | solution.py:24
  37.4 8.3 %collective-permute-start.16 = (f32[128,512]{1,0:T(8,128)S(1)}, f32[128,512]{1,0:T(8,128)S(1)}, u32[]{:S(2)}, u32[]{:S(2)}) collective-permute-start(f32[128,512]{1,0:T(8,128)S(1)} %collective-permute-done.7.refs_2_), channel_id=1, source_target_pairs={{0,1},{1,0},{2,3},{3,2},{4,5},{5,4},{6,7},{7,6},{8,9},{9,8},{10,11... | collective-permute-start | bytes 786440 | tf_op jit(solution)/shard_map/ppermute | solution.py:24
  38.8 6.9 %collective-permute-start.17 = (f32[128,512]{1,0:T(8,128)S(1)}, f32[128,512]{1,0:T(8,128)S(1)}, u32[]{:S(2)}, u32[]{:S(2)}) collective-permute-start(f32[128,512]{1,0:T(8,128)S(1)} %collective-permute-done.10.refs_3_), channel_id=1, source_target_pairs={{0,1},{1,0},{2,3},{3,2},{4,5},{5,4},{6,7},{7,6},{8,9},{9,8},{10,11... | collective-permute-start | bytes 786440 | tf_op jit(solution)/shard_map/ppermute | solution.py:24
  41.0 3.0 %copy-start.2 = (f32[2,64,512]{2,1,0:T(8,128)}, f32[2,64,512]{2,1,0:T(8,128)S(1)}, u32[]{:S(2)}) copy-start(f32[2,64,512]{2,1,0:T(8,128)S(1)} %collective-permute-done.12.refs_7_) | copy-start | bytes 786436
  41.0 4.7 %collective-permute-start.15 = (f32[128,512]{1,0:T(8,128)S(1)}, f32[128,512]{1,0:T(8,128)S(1)}, u32[]{:S(2)}, u32[]{:S(2)}) collective-permute-start(f32[128,512]{1,0:T(8,128)S(1)} %collective-permute-done.13.refs_1_), channel_id=1, source_target_pairs={{0,1},{1,0},{2,3},{3,2},{4,5},{5,4},{6,7},{7,6},{8,9},{9,8},{10,11... | collective-permute-start | bytes 786440 | tf_op jit(solution)/shard_map/ppermute | solution.py:24
  44.0 0.9 %slice-start = ((f32[2,64,512]{2,1,0:T(8,128)}), f32[1,64,512]{2,1,0:T(8,128)S(1)}, s32[]{:S(2)}) async-start(f32[2,64,512]{2,1,0:T(8,128)} %copy-done.2), calls=%async_computation | async-start | bytes 262144 | tf_op jit(solution)/shard_map/slice | solution.py:241
  44.9 1.4 %copy-start.3 = (f32[2,64,512]{2,1,0:T(8,128)S(1)}, f32[2,64,512]{2,1,0:T(8,128)}, u32[]{:S(2)}) copy-start(f32[2,64,512]{2,1,0:T(8,128)} %copy-done.2) | copy-start | bytes 786436
  45.0 5.8 %collective-permute-start.18 = (f32[2,64,512]{2,1,0:T(8,128)S(1)}, f32[2,64,512]{2,1,0:T(8,128)S(1)}, u32[]{:S(2)}, u32[]{:S(2)}) collective-permute-start(f32[2,64,512]{2,1,0:T(8,128)S(1)} %pad_maximum_fusion.2), channel_id=1, source_target_pairs={{0,2},{1,15},{2,4},{3,1},{4,6},{5,3},{6,8},{7,5},{8,10},{9,7},{10,... | collective-permute-start | bytes 786440 | tf_op jit(solution)/shard_map/ppermute | solution.py:24
  48.0 7.1 %collective-permute-start.19 = (f32[7,64,256]{2,1,0:T(8,128)S(1)}, f32[7,64,256]{2,1,0:T(8,128)S(1)}, u32[]{:S(2)}, u32[]{:S(2)}) collective-permute-start(f32[7,64,256]{2,1,0:T(8,128)S(1)} %get-tuple-element.49), channel_id=1, source_target_pairs={{0,1},{1,0},{2,3},{3,2},{4,5},{5,4},{6,7},{7,6},{8,9},{9,8},{10,11... | collective-permute-start | bytes 1376264 | tf_op jit(solution)/shard_map/ppermute | solution.py:24
  51.4 3.7 %collective-permute-start.20 = (f32[1,64,256]{2,1,0:T(8,128)S(1)}, f32[1,64,256]{2,1,0:T(8,128)S(1)}, u32[]{:S(2)}, u32[]{:S(2)}) collective-permute-start(f32[1,64,256]{2,1,0:T(8,128)S(1)} %get-tuple-element.50), channel_id=1, source_target_pairs={{0,1},{1,0},{2,3},{3,2},{4,5},{5,4},{6,7},{7,6},{8,9},{9,8},{10,11... | collective-permute-start | bytes 196616 | tf_op jit(solution)/shard_map/ppermute | solution.py:24
  55.7 7.0 %collective-permute-start.23 = (f32[2,64,256]{2,1,0:T(8,128)S(1)}, f32[2,64,256]{2,1,0:T(8,128)S(1)}, u32[]{:S(2)}, u32[]{:S(2)}) collective-permute-start(f32[2,64,256]{2,1,0:T(8,128)S(1)} %get-tuple-element.54), channel_id=1, source_target_pairs={{0,192},{1,193},{2,194},{3,195},{4,196},{5,197},{6,198},{7,199},{8... | collective-permute-start | bytes 393224 | tf_op jit(solution)/shard_map/ppermute | solution.py:24
  58.3 5.9 %collective-permute-start.22 = (f32[2,64,256]{2,1,0:T(8,128)S(1)}, f32[2,64,256]{2,1,0:T(8,128)S(1)}, u32[]{:S(2)}, u32[]{:S(2)}) collective-permute-start(f32[2,64,256]{2,1,0:T(8,128)S(1)} %get-tuple-element.53), channel_id=1, source_target_pairs={{0,128},{1,129},{2,130},{3,131},{4,132},{5,133},{6,134},{7,135},{8... | collective-permute-start | bytes 393224 | tf_op jit(solution)/shard_map/ppermute | solution.py:24
  58.8 10.3 %collective-permute-start.21 = (f32[2,64,256]{2,1,0:T(8,128)S(1)}, f32[2,64,256]{2,1,0:T(8,128)S(1)}, u32[]{:S(2)}, u32[]{:S(2)}) collective-permute-start(f32[2,64,256]{2,1,0:T(8,128)S(1)} %get-tuple-element.52), channel_id=1, source_target_pairs={{0,64},{1,65},{2,66},{3,67},{4,68},{5,69},{6,70},{7,71},{8,72},{9,... | collective-permute-start | bytes 393224 | tf_op jit(solution)/shard_map/ppermute | solution.py:24
  59.4 13.3 %collective-permute-start.27 = (f32[2,64,256]{2,1,0:T(8,128)S(1)}, f32[2,64,256]{2,1,0:T(8,128)S(1)}, u32[]{:S(2)}, u32[]{:S(2)}) collective-permute-start(f32[2,64,256]{2,1,0:T(8,128)S(1)} %get-tuple-element.58), channel_id=1, source_target_pairs={{0,192},{1,193},{2,194},{3,195},{4,196},{5,197},{6,198},{7,199},{8... | collective-permute-start | bytes 393224 | tf_op jit(solution)/shard_map/ppermute | solution.py:24
  61.4 11.2 %collective-permute-start.26 = (f32[2,64,256]{2,1,0:T(8,128)S(1)}, f32[2,64,256]{2,1,0:T(8,128)S(1)}, u32[]{:S(2)}, u32[]{:S(2)}) collective-permute-start(f32[2,64,256]{2,1,0:T(8,128)S(1)} %get-tuple-element.57), channel_id=1, source_target_pairs={{0,128},{1,129},{2,130},{3,131},{4,132},{5,133},{6,134},{7,135},{8... | collective-permute-start | bytes 393224 | tf_op jit(solution)/shard_map/ppermute | solution.py:24
  62.7 10.6 %collective-permute-start.25 = (f32[2,64,256]{2,1,0:T(8,128)S(1)}, f32[2,64,256]{2,1,0:T(8,128)S(1)}, u32[]{:S(2)}, u32[]{:S(2)}) collective-permute-start(f32[2,64,256]{2,1,0:T(8,128)S(1)} %get-tuple-element.56), channel_id=1, source_target_pairs={{0,64},{1,65},{2,66},{3,67},{4,68},{5,69},{6,70},{7,71},{8,72},{9,... | collective-permute-start | bytes 393224 | tf_op jit(solution)/shard_map/ppermute | solution.py:24
  69.1 7.7 %collective-permute-start.24 = (f32[2,64,256]{2,1,0:T(8,128)S(1)}, f32[2,64,256]{2,1,0:T(8,128)S(1)}, u32[]{:S(2)}, u32[]{:S(2)}) collective-permute-start(f32[2,64,256]{2,1,0:T(8,128)S(1)} %add_add_fusion.1), channel_id=1, source_target_pairs={{0,32},{1,48},{2,34},{3,50},{4,36},{5,52},{6,38},{7,54},{8,40},{9,... | collective-permute-start | bytes 393224 | tf_op jit(solution)/shard_map/ppermute | solution.py:24
  73.3 7.7 %copy-start.5 = (s32[2,16]{1,0:T(2,128)S(1)}, s32[2,16]{1,0:T(2,128)}, u32[]{:S(2)}) copy-start(s32[2,16]{1,0:T(2,128)} %pattern_ref.7) | copy-start | bytes 388
  73.3 6.3 %collective-permute-start.28 = (f32[2,64,256]{2,1,0:T(8,128)S(1)}, f32[2,64,256]{2,1,0:T(8,128)S(1)}, u32[]{:S(2)}, u32[]{:S(2)}) collective-permute-start(f32[2,64,256]{2,1,0:T(8,128)S(1)} %add_add_fusion), channel_id=1, source_target_pairs={{0,0},{1,16},{2,2},{3,18},{4,4},{5,20},{6,6},{7,22},{8,8},{9,24},{... | collective-permute-start | bytes 393224 | tf_op jit(solution)/shard_map/ppermute | solution.py:24
  76.7 2.9 %collective-permute-start.29 = (f32[2,64,256]{2,1,0:T(8,128)S(1)}, f32[2,64,256]{2,1,0:T(8,128)S(1)}, u32[]{:S(2)}, u32[]{:S(2)}) collective-permute-start(f32[2,64,256]{2,1,0:T(8,128)S(1)} %collective-permute-done.24.own_flip), channel_id=1, source_target_pairs={{0,1},{1,0},{2,3},{3,2},{4,5},{5,4},{6,7},{7,6},{8,9},{9,8},{10,11... | collective-permute-start | bytes 393224 | tf_op jit(solution)/shard_map/ppermute | solution.py:24
  79.6 1.3 %collective-permute-start.30 = (f32[2,64,256]{2,1,0:T(8,128)S(1)}, f32[2,64,256]{2,1,0:T(8,128)S(1)}, u32[]{:S(2)}, u32[]{:S(2)}) collective-permute-start(f32[2,64,256]{2,1,0:T(8,128)S(1)} %collective-permute-done.28.own_same), channel_id=1, source_target_pairs={{0,1},{1,0},{2,3},{3,2},{4,5},{5,4},{6,7},{7,6},{8,9},{9,8},{10,11... | collective-permute-start | bytes 393224 | tf_op jit(solution)/shard_map/ppermute | solution.py:24
